TPU v7x, 256 devices: a whole 4x4x8 slice. The times are simulated.
256 devices in a mesh: row: 32 (over z, y_hi, core), col: 8 (over x, y_lo).
Axes of the slice: x: 4, y: 4 (y_hi: 2, y_lo: 2; y = y_hi * 2 + y_lo), z: 8, core: 2. Of those that a mesh axis runs over, the one named last changes fastest.
Arguments:
- gradient: bfloat16 [8192, 14336], P('row', 'col'), may hold values from -6 to 6
Outputs:
- statistics: float32 [8192, 8192], P(('row', 'col'))
All inputs are finite; a program needn't handle non-finite values.
Results may differ from a plain program's by a relative error of at most 0.0003.
Values may be sent and summed in bfloat16 or wider, within the bound.
No kernel may reach another device: no remote copies, remote signals or barrier semaphores. Data moves between devices by JAX's collectives and lax.ppermute only.
A program may use at most 64 MiB of HBM per device.

v0:
```python
import jax
import jax.numpy as jnp
import numpy as np
from jax import lax
from jax.sharding import PartitionSpec as P

NCOL = 14336


def from_behind(value, axis, steps):
    count = lax.axis_size(axis)
    pairs = [(source, (source + steps) % count) for source in range(count)]
    return lax.ppermute(value, axis, pairs)


def product(gradient, visiting):
    return lax.dot_general(
        gradient, visiting, (((1,), (1,)), ((), ())), preferred_element_type=jnp.float32
    )


def advance(block):
    return from_behind(block, "row", 1)


def return_tiles(mirrors, half):
    for bit in range((half - 1).bit_length()):
        picked = np.array([dist - 1 for dist in range(1, half) if dist >> bit & 1], dtype=np.int32)
        moved = from_behind(mirrors[picked], "row", -(1 << bit))
        mirrors = mirrors.at[picked].set(moved)
    return mirrors


def place_mirrors(whole, mirrors, myself, nrow, rows, half):

    def put(dist, acc):
        start = (myself + dist) % nrow * rows
        return lax.dynamic_update_slice(acc, mirrors[dist - 1], (jnp.int32(0), start))

    return lax.fori_loop(1, half, put, whole)


def per_device(gradient):
    rows = gradient.shape[0]
    nrow = lax.axis_size("row")
    half = nrow // 2
    myself = lax.axis_index("row")
    width = rows * nrow

    def block_start(dist):
        return (myself - dist) % nrow * rows

    zero = jnp.int32(0)
    whole = jnp.zeros((rows, width), jnp.float32)
    whole = lax.dynamic_update_slice(whole, product(gradient, gradient), (zero, block_start(0)))
    mirrors = jnp.zeros((half - 1, rows, rows), jnp.float32)

    def step(dist, carry):
        block, acc, store = carry
        block = advance(block)
        tile = product(gradient, block)
        acc = lax.dynamic_update_slice(acc, tile, (zero, block_start(dist)))
        store = lax.dynamic_update_index_in_dim(store, tile.T, dist - 1, 0)
        return (block, acc, store)

    block, whole, mirrors = lax.fori_loop(1, half, step, (gradient, whole, mirrors))
    block = advance(block)
    whole = lax.dynamic_update_slice(whole, product(gradient, block), (zero, block_start(half)))
    mirrors = return_tiles(mirrors, half)
    whole = place_mirrors(whole, mirrors, myself, nrow, rows, half)
    summed = lax.psum_scatter(whole, "col", scatter_dimension=0, tiled=True)
    return summed / NCOL


def solution(mesh):
    return jax.shard_map(
        per_device,
        mesh=mesh,
        in_specs=(P("row", "col"),),
        out_specs=P(("row", "col"), None),
        check_vma=False,
    )
```

profile of v0, /device:TPU:32, one launch (start us, length us, event | category | flops | bytes accessed | tf_op | source)
XLA Modules:
  0.0 738.8 jit_solution(14192905941607757684)
XLA Ops:
  12.6 261.1 %while.38 = (s32[]{:T(128)}, bf16[256,1792]{1,0:T(8,128)(2,1)S(1)}, f32[256,8192]{1,0:T(8,128)}, f32[15,256,256]{2,1,0:T(8,128)}, bf16[256,1792]{1,0:T(8,128)(2,...) while((s32[]{:T(128)}, bf16[256,1792]{1,0:T(8,128)(2,1)S(1)}, ...), condition=%wide.region_1.2_spmd, body=%wide.region_0.1_spmd.sunk | while | flops 234881040 | bytes 8913236 | solution.py:66
  12.6 15.2 %collective-permute-done = bf16[256,1792]{1,0:T(8,128)(2,1)S(1)} collective-permute-done((bf16[256,1792]{1,0:T(8,128)(2,1)S(1)}, bf16[256,1792]{1,0:T(8,128)(2,1)S(1)}, u32[]{:S(2)}, u32[]{:S(2)}) %collective-permute-start) | collective-permute-done | bytes 917536 | tf_op jit(solution)/shard_map/while/body/eval_jaxpr/ppermute | solution.py:13
  30.1 15.2 %collective-permute-done = bf16[256,1792]{1,0:T(8,128)(2,1)S(1)} collective-permute-done((bf16[256,1792]{1,0:T(8,128)(2,1)S(1)}, bf16[256,1792]{1,0:T(8,128)(2,1)S(1)}, u32[]{:S(2)}, u32[]{:S(2)}) %collective-permute-start) | collective-permute-done | bytes 917536 | tf_op jit(solution)/shard_map/while/body/eval_jaxpr/ppermute | solution.py:13
  47.5 15.2 %collective-permute-done = bf16[256,1792]{1,0:T(8,128)(2,1)S(1)} collective-permute-done((bf16[256,1792]{1,0:T(8,128)(2,1)S(1)}, bf16[256,1792]{1,0:T(8,128)(2,1)S(1)}, u32[]{:S(2)}, u32[]{:S(2)}) %collective-permute-start) | collective-permute-done | bytes 917536 | tf_op jit(solution)/shard_map/while/body/eval_jaxpr/ppermute | solution.py:13
  64.9 15.2 %collective-permute-done = bf16[256,1792]{1,0:T(8,128)(2,1)S(1)} collective-permute-done((bf16[256,1792]{1,0:T(8,128)(2,1)S(1)}, bf16[256,1792]{1,0:T(8,128)(2,1)S(1)}, u32[]{:S(2)}, u32[]{:S(2)}) %collective-permute-start) | collective-permute-done | bytes 917536 | tf_op jit(solution)/shard_map/while/body/eval_jaxpr/ppermute | solution.py:13
  82.4 15.2 %collective-permute-done = bf16[256,1792]{1,0:T(8,128)(2,1)S(1)} collective-permute-done((bf16[256,1792]{1,0:T(8,128)(2,1)S(1)}, bf16[256,1792]{1,0:T(8,128)(2,1)S(1)}, u32[]{:S(2)}, u32[]{:S(2)}) %collective-permute-start) | collective-permute-done | bytes 917536 | tf_op jit(solution)/shard_map/while/body/eval_jaxpr/ppermute | solution.py:13
  99.8 15.2 %collective-permute-done = bf16[256,1792]{1,0:T(8,128)(2,1)S(1)} collective-permute-done((bf16[256,1792]{1,0:T(8,128)(2,1)S(1)}, bf16[256,1792]{1,0:T(8,128)(2,1)S(1)}, u32[]{:S(2)}, u32[]{:S(2)}) %collective-permute-start) | collective-permute-done | bytes 917536 | tf_op jit(solution)/shard_map/while/body/eval_jaxpr/ppermute | solution.py:13
  117.2 15.2 %collective-permute-done = bf16[256,1792]{1,0:T(8,128)(2,1)S(1)} collective-permute-done((bf16[256,1792]{1,0:T(8,128)(2,1)S(1)}, bf16[256,1792]{1,0:T(8,128)(2,1)S(1)}, u32[]{:S(2)}, u32[]{:S(2)}) %collective-permute-start) | collective-permute-done | bytes 917536 | tf_op jit(solution)/shard_map/while/body/eval_jaxpr/ppermute | solution.py:13
  134.6 15.2 %collective-permute-done = bf16[256,1792]{1,0:T(8,128)(2,1)S(1)} collective-permute-done((bf16[256,1792]{1,0:T(8,128)(2,1)S(1)}, bf16[256,1792]{1,0:T(8,128)(2,1)S(1)}, u32[]{:S(2)}, u32[]{:S(2)}) %collective-permute-start) | collective-permute-done | bytes 917536 | tf_op jit(solution)/shard_map/while/body/eval_jaxpr/ppermute | solution.py:13
  152.0 15.2 %collective-permute-done = bf16[256,1792]{1,0:T(8,128)(2,1)S(1)} collective-permute-done((bf16[256,1792]{1,0:T(8,128)(2,1)S(1)}, bf16[256,1792]{1,0:T(8,128)(2,1)S(1)}, u32[]{:S(2)}, u32[]{:S(2)}) %collective-permute-start) | collective-permute-done | bytes 917536 | tf_op jit(solution)/shard_map/while/body/eval_jaxpr/ppermute | solution.py:13
  169.4 15.2 %collective-permute-done = bf16[256,1792]{1,0:T(8,128)(2,1)S(1)} collective-permute-done((bf16[256,1792]{1,0:T(8,128)(2,1)S(1)}, bf16[256,1792]{1,0:T(8,128)(2,1)S(1)}, u32[]{:S(2)}, u32[]{:S(2)}) %collective-permute-start) | collective-permute-done | bytes 917536 | tf_op jit(solution)/shard_map/while/body/eval_jaxpr/ppermute | solution.py:13
  186.7 15.2 %collective-permute-done = bf16[256,1792]{1,0:T(8,128)(2,1)S(1)} collective-permute-done((bf16[256,1792]{1,0:T(8,128)(2,1)S(1)}, bf16[256,1792]{1,0:T(8,128)(2,1)S(1)}, u32[]{:S(2)}, u32[]{:S(2)}) %collective-permute-start) | collective-permute-done | bytes 917536 | tf_op jit(solution)/shard_map/while/body/eval_jaxpr/ppermute | solution.py:13
  204.1 15.2 %collective-permute-done = bf16[256,1792]{1,0:T(8,128)(2,1)S(1)} collective-permute-done((bf16[256,1792]{1,0:T(8,128)(2,1)S(1)}, bf16[256,1792]{1,0:T(8,128)(2,1)S(1)}, u32[]{:S(2)}, u32[]{:S(2)}) %collective-permute-start) | collective-permute-done | bytes 917536 | tf_op jit(solution)/shard_map/while/body/eval_jaxpr/ppermute | solution.py:13
  221.5 15.2 %collective-permute-done = bf16[256,1792]{1,0:T(8,128)(2,1)S(1)} collective-permute-done((bf16[256,1792]{1,0:T(8,128)(2,1)S(1)}, bf16[256,1792]{1,0:T(8,128)(2,1)S(1)}, u32[]{:S(2)}, u32[]{:S(2)}) %collective-permute-start) | collective-permute-done | bytes 917536 | tf_op jit(solution)/shard_map/while/body/eval_jaxpr/ppermute | solution.py:13
  239.0 15.2 %collective-permute-done = bf16[256,1792]{1,0:T(8,128)(2,1)S(1)} collective-permute-done((bf16[256,1792]{1,0:T(8,128)(2,1)S(1)}, bf16[256,1792]{1,0:T(8,128)(2,1)S(1)}, u32[]{:S(2)}, u32[]{:S(2)}) %collective-permute-start) | collective-permute-done | bytes 917536 | tf_op jit(solution)/shard_map/while/body/eval_jaxpr/ppermute | solution.py:13
  256.3 15.3 %collective-permute-done = bf16[256,1792]{1,0:T(8,128)(2,1)S(1)} collective-permute-done((bf16[256,1792]{1,0:T(8,128)(2,1)S(1)}, bf16[256,1792]{1,0:T(8,128)(2,1)S(1)}, u32[]{:S(2)}, u32[]{:S(2)}) %collective-permute-start) | collective-permute-done | bytes 917536 | tf_op jit(solution)/shard_map/while/body/eval_jaxpr/ppermute | solution.py:13
  278.8 23.8 %collective-permute-done.2 = f32[8,256,256]{2,1,0:T(8,128)S(1)} collective-permute-done((f32[8,256,256]{2,1,0:T(8,128)}, f32[8,256,256]{2,1,0:T(8,128)S(1)}, u32[]{:S(2)}, u32[]{:S(2)}) %collective-permute-start.2) | collective-permute-done | bytes 2097184 | tf_op jit(solution)/shard_map/ppermute | solution.py:13
  321.5 38.7 %collective-permute-done.3 = f32[8,256,256]{2,1,0:T(8,128)S(1)} collective-permute-done((f32[8,256,256]{2,1,0:T(8,128)}, f32[8,256,256]{2,1,0:T(8,128)S(1)}, u32[]{:S(2)}, u32[]{:S(2)}) %collective-permute-start.3) | collective-permute-done | bytes 2097184 | tf_op jit(solution)/shard_map/ppermute | solution.py:13
  367.9 12.3 %collective-permute-start.4 = (f32[8,256,256]{2,1,0:T(8,128)}, f32[8,256,256]{2,1,0:T(8,128)S(1)}, u32[]{:S(2)}, u32[]{:S(2)}) collective-permute-start(f32[8,256,256]{2,1,0:T(8,128)} %gather_fusion.2), channel_id=1, source_target_pairs={{0,224},{8,232},{16,240},{24,248},{32,0},{40,8},{48,16},{56,24},{6... | collective-permute-start | bytes 6291464 | tf_op jit(solution)/shard_map/ppermute | solution.py:13
  380.2 42.2 %collective-permute-done.4 = f32[8,256,256]{2,1,0:T(8,128)S(1)} collective-permute-done((f32[8,256,256]{2,1,0:T(8,128)}, f32[8,256,256]{2,1,0:T(8,128)S(1)}, u32[]{:S(2)}, u32[]{:S(2)}) %collective-permute-start.4) | collective-permute-done | bytes 2097184 | tf_op jit(solution)/shard_map/ppermute | solution.py:13
  436.7 15.8 %collective-permute-done.1 = bf16[256,1792]{1,0:T(8,128)(2,1)} collective-permute-done((bf16[256,1792]{1,0:T(8,128)(2,1)}, bf16[256,1792]{1,0:T(8,128)(2,1)}, u32[]{:S(2)}, u32[]{:S(2)}) %collective-permute-start.1) | collective-permute-done | bytes 917536 | tf_op jit(solution)/shard_map/ppermute | solution.py:13
  455.0 54.9 %collective-permute-done.5 = f32[8,256,256]{2,1,0:T(8,128)S(1)} collective-permute-done((f32[8,256,256]{2,1,0:T(8,128)}, f32[8,256,256]{2,1,0:T(8,128)S(1)}, u32[]{:S(2)}, u32[]{:S(2)}) %collective-permute-start.5) | collective-permute-done | bytes 2097184 | tf_op jit(solution)/shard_map/ppermute | solution.py:13
  513.4 25.4 %while.39 = (s32[]{:T(128)}, f32[256,8192]{1,0:T(8,128)}, f32[15,256,256]{2,1,0:T(8,128)}, s32[]{:T(128)}, s32[]{:T(128)}, /*index=5*/s32[]{:T(128)}, s32[]{:T(128)}, s32[]{:T(128)}, s32[]{:T(128)}, s32[]{:T(128)}) while((s32[]{:T(128)}, f32[256,8192]{1,0:T(8,128)}, f32[15,256,256]{2,1,0:T(8,128)}, s32[]{:T(128)}, s32[]{:T(128)}, ...), condition=%wide.region_7.8_spmd, body=%wide.region_6.7_spmd.sunk | while | flops 18 | bytes 525080 | solution.py:40
  538.9 190.8 %reduce-scatter.2.cloned.1.call-done = f32[32,8192]{1,0:T(8,128)} async-done(((f32[256,8192]{1,0:T(8,128)}), f32[32,8192]{1,0:T(8,128)}) %reduce-scatter.2.cloned.1.call-update) | async-done | bytes 1048592 | tf_op jit(solution)/shard_map/reduce_scatter | solution.py:71
  (129 shorter events, 118.0 us)
Async XLA Ops:
  6.5 723.1 %reduce-scatter.2.cloned.1.call-start = ((), (), s32[]{:S(2)}) async-start(), calls=%async_computation.1 | async-start | bytes 9437184 | tf_op jit(solution)/shard_map/reduce_scatter | solution.py:71
  12.6 15.2 %collective-permute-start = (bf16[256,1792]{1,0:T(8,128)(2,1)S(1)}, bf16[256,1792]{1,0:T(8,128)(2,1)S(1)}, u32[]{:S(2)}, u32[]{:S(2)}) collective-permute-start(bf16[256,1792]{1,0:T(8,128)(2,1)S(1)} %get-tuple-element.456), channel_id=1, source_target_pairs={{0,8},{8,16},{16,24},{24,32},{32,40},{40,48},{48,56},{56,64},{64,7... | collective-permute-start | bytes 2752520 | tf_op jit(solution)/shard_map/while/body/eval_jaxpr/ppermute | solution.py:13
  29.9 15.3 %collective-permute-start = (bf16[256,1792]{1,0:T(8,128)(2,1)S(1)}, bf16[256,1792]{1,0:T(8,128)(2,1)S(1)}, u32[]{:S(2)}, u32[]{:S(2)}) collective-permute-start(bf16[256,1792]{1,0:T(8,128)(2,1)S(1)} %get-tuple-element.456), channel_id=1, source_target_pairs={{0,8},{8,16},{16,24},{24,32},{32,40},{40,48},{48,56},{56,64},{64,7... | collective-permute-start | bytes 2752520 | tf_op jit(solution)/shard_map/while/body/eval_jaxpr/ppermute | solution.py:13
  47.4 15.3 %collective-permute-start = (bf16[256,1792]{1,0:T(8,128)(2,1)S(1)}, bf16[256,1792]{1,0:T(8,128)(2,1)S(1)}, u32[]{:S(2)}, u32[]{:S(2)}) collective-permute-start(bf16[256,1792]{1,0:T(8,128)(2,1)S(1)} %get-tuple-element.456), channel_id=1, source_target_pairs={{0,8},{8,16},{16,24},{24,32},{32,40},{40,48},{48,56},{56,64},{64,7... | collective-permute-start | bytes 2752520 | tf_op jit(solution)/shard_map/while/body/eval_jaxpr/ppermute | solution.py:13
  64.8 15.3 %collective-permute-start = (bf16[256,1792]{1,0:T(8,128)(2,1)S(1)}, bf16[256,1792]{1,0:T(8,128)(2,1)S(1)}, u32[]{:S(2)}, u32[]{:S(2)}) collective-permute-start(bf16[256,1792]{1,0:T(8,128)(2,1)S(1)} %get-tuple-element.456), channel_id=1, source_target_pairs={{0,8},{8,16},{16,24},{24,32},{32,40},{40,48},{48,56},{56,64},{64,7... | collective-permute-start | bytes 2752520 | tf_op jit(solution)/shard_map/while/body/eval_jaxpr/ppermute | solution.py:13
  82.3 15.3 %collective-permute-start = (bf16[256,1792]{1,0:T(8,128)(2,1)S(1)}, bf16[256,1792]{1,0:T(8,128)(2,1)S(1)}, u32[]{:S(2)}, u32[]{:S(2)}) collective-permute-start(bf16[256,1792]{1,0:T(8,128)(2,1)S(1)} %get-tuple-element.456), channel_id=1, source_target_pairs={{0,8},{8,16},{16,24},{24,32},{32,40},{40,48},{48,56},{56,64},{64,7... | collective-permute-start | bytes 2752520 | tf_op jit(solution)/shard_map/while/body/eval_jaxpr/ppermute | solution.py:13
  99.6 15.3 %collective-permute-start = (bf16[256,1792]{1,0:T(8,128)(2,1)S(1)}, bf16[256,1792]{1,0:T(8,128)(2,1)S(1)}, u32[]{:S(2)}, u32[]{:S(2)}) collective-permute-start(bf16[256,1792]{1,0:T(8,128)(2,1)S(1)} %get-tuple-element.456), channel_id=1, source_target_pairs={{0,8},{8,16},{16,24},{24,32},{32,40},{40,48},{48,56},{56,64},{64,7... | collective-permute-start | bytes 2752520 | tf_op jit(solution)/shard_map/while/body/eval_jaxpr/ppermute | solution.py:13
  117.0 15.3 %collective-permute-start = (bf16[256,1792]{1,0:T(8,128)(2,1)S(1)}, bf16[256,1792]{1,0:T(8,128)(2,1)S(1)}, u32[]{:S(2)}, u32[]{:S(2)}) collective-permute-start(bf16[256,1792]{1,0:T(8,128)(2,1)S(1)} %get-tuple-element.456), channel_id=1, source_target_pairs={{0,8},{8,16},{16,24},{24,32},{32,40},{40,48},{48,56},{56,64},{64,7... | collective-permute-start | bytes 2752520 | tf_op jit(solution)/shard_map/while/body/eval_jaxpr/ppermute | solution.py:13
  134.4 15.3 %collective-permute-start = (bf16[256,1792]{1,0:T(8,128)(2,1)S(1)}, bf16[256,1792]{1,0:T(8,128)(2,1)S(1)}, u32[]{:S(2)}, u32[]{:S(2)}) collective-permute-start(bf16[256,1792]{1,0:T(8,128)(2,1)S(1)} %get-tuple-element.456), channel_id=1, source_target_pairs={{0,8},{8,16},{16,24},{24,32},{32,40},{40,48},{48,56},{56,64},{64,7... | collective-permute-start | bytes 2752520 | tf_op jit(solution)/shard_map/while/body/eval_jaxpr/ppermute | solution.py:13
  151.9 15.3 %collective-permute-start = (bf16[256,1792]{1,0:T(8,128)(2,1)S(1)}, bf16[256,1792]{1,0:T(8,128)(2,1)S(1)}, u32[]{:S(2)}, u32[]{:S(2)}) collective-permute-start(bf16[256,1792]{1,0:T(8,128)(2,1)S(1)} %get-tuple-element.456), channel_id=1, source_target_pairs={{0,8},{8,16},{16,24},{24,32},{32,40},{40,48},{48,56},{56,64},{64,7... | collective-permute-start | bytes 2752520 | tf_op jit(solution)/shard_map/while/body/eval_jaxpr/ppermute | solution.py:13
  169.3 15.3 %collective-permute-start = (bf16[256,1792]{1,0:T(8,128)(2,1)S(1)}, bf16[256,1792]{1,0:T(8,128)(2,1)S(1)}, u32[]{:S(2)}, u32[]{:S(2)}) collective-permute-start(bf16[256,1792]{1,0:T(8,128)(2,1)S(1)} %get-tuple-element.456), channel_id=1, source_target_pairs={{0,8},{8,16},{16,24},{24,32},{32,40},{40,48},{48,56},{56,64},{64,7... | collective-permute-start | bytes 2752520 | tf_op jit(solution)/shard_map/while/body/eval_jaxpr/ppermute | solution.py:13
  186.6 15.3 %collective-permute-start = (bf16[256,1792]{1,0:T(8,128)(2,1)S(1)}, bf16[256,1792]{1,0:T(8,128)(2,1)S(1)}, u32[]{:S(2)}, u32[]{:S(2)}) collective-permute-start(bf16[256,1792]{1,0:T(8,128)(2,1)S(1)} %get-tuple-element.456), channel_id=1, source_target_pairs={{0,8},{8,16},{16,24},{24,32},{32,40},{40,48},{48,56},{56,64},{64,7... | collective-permute-start | bytes 2752520 | tf_op jit(solution)/shard_map/while/body/eval_jaxpr/ppermute | solution.py:13
  204.0 15.3 %collective-permute-start = (bf16[256,1792]{1,0:T(8,128)(2,1)S(1)}, bf16[256,1792]{1,0:T(8,128)(2,1)S(1)}, u32[]{:S(2)}, u32[]{:S(2)}) collective-permute-start(bf16[256,1792]{1,0:T(8,128)(2,1)S(1)} %get-tuple-element.456), channel_id=1, source_target_pairs={{0,8},{8,16},{16,24},{24,32},{32,40},{40,48},{48,56},{56,64},{64,7... | collective-permute-start | bytes 2752520 | tf_op jit(solution)/shard_map/while/body/eval_jaxpr/ppermute | solution.py:13
  221.4 15.3 %collective-permute-start = (bf16[256,1792]{1,0:T(8,128)(2,1)S(1)}, bf16[256,1792]{1,0:T(8,128)(2,1)S(1)}, u32[]{:S(2)}, u32[]{:S(2)}) collective-permute-start(bf16[256,1792]{1,0:T(8,128)(2,1)S(1)} %get-tuple-element.456), channel_id=1, source_target_pairs={{0,8},{8,16},{16,24},{24,32},{32,40},{40,48},{48,56},{56,64},{64,7... | collective-permute-start | bytes 2752520 | tf_op jit(solution)/shard_map/while/body/eval_jaxpr/ppermute | solution.py:13
  238.8 15.3 %collective-permute-start = (bf16[256,1792]{1,0:T(8,128)(2,1)S(1)}, bf16[256,1792]{1,0:T(8,128)(2,1)S(1)}, u32[]{:S(2)}, u32[]{:S(2)}) collective-permute-start(bf16[256,1792]{1,0:T(8,128)(2,1)S(1)} %get-tuple-element.456), channel_id=1, source_target_pairs={{0,8},{8,16},{16,24},{24,32},{32,40},{40,48},{48,56},{56,64},{64,7... | collective-permute-start | bytes 2752520 | tf_op jit(solution)/shard_map/while/body/eval_jaxpr/ppermute | solution.py:13
  256.2 15.4 %collective-permute-start = (bf16[256,1792]{1,0:T(8,128)(2,1)S(1)}, bf16[256,1792]{1,0:T(8,128)(2,1)S(1)}, u32[]{:S(2)}, u32[]{:S(2)}) collective-permute-start(bf16[256,1792]{1,0:T(8,128)(2,1)S(1)} %get-tuple-element.456), channel_id=1, source_target_pairs={{0,8},{8,16},{16,24},{24,32},{32,40},{40,48},{48,56},{56,64},{64,7... | collective-permute-start | bytes 2752520 | tf_op jit(solution)/shard_map/while/body/eval_jaxpr/ppermute | solution.py:13
  273.7 5.1 copy-start.5
  278.8 23.9 %collective-permute-start.2 = (f32[8,256,256]{2,1,0:T(8,128)}, f32[8,256,256]{2,1,0:T(8,128)S(1)}, u32[]{:S(2)}, u32[]{:S(2)}) collective-permute-start(f32[8,256,256]{2,1,0:T(8,128)} %gather_fusion), channel_id=1, source_target_pairs={{0,248},{8,0},{16,8},{24,16},{32,24},{40,32},{48,40},{56,48},{64,5... | collective-permute-start | bytes 6291464 | tf_op jit(solution)/shard_map/ppermute | solution.py:13
  278.8 42.7 %copy-start.4 = (s32[8]{0:T(128)S(1)}, s32[8]{0:T(128)}, u32[]{:S(2)}) copy-start(s32[8]{0:T(128)} %constant.256) | copy-start | bytes 100
  310.3 50.0 %collective-permute-start.3 = (f32[8,256,256]{2,1,0:T(8,128)}, f32[8,256,256]{2,1,0:T(8,128)S(1)}, u32[]{:S(2)}, u32[]{:S(2)}) collective-permute-start(f32[8,256,256]{2,1,0:T(8,128)} %gather_fusion.1), channel_id=1, source_target_pairs={{0,240},{8,248},{16,0},{24,8},{32,16},{40,24},{48,32},{56,40},{64,... | collective-permute-start | bytes 6291464 | tf_op jit(solution)/shard_map/ppermute | solution.py:13
  321.5 58.7 %copy-start.3 = (s32[8]{0:T(128)S(1)}, s32[8]{0:T(128)}, u32[]{:S(2)}) copy-start(s32[8]{0:T(128)} %constant.258) | copy-start | bytes 100
  367.9 54.5 %collective-permute-start.4 = (f32[8,256,256]{2,1,0:T(8,128)}, f32[8,256,256]{2,1,0:T(8,128)S(1)}, u32[]{:S(2)}, u32[]{:S(2)}) collective-permute-start(f32[8,256,256]{2,1,0:T(8,128)} %gather_fusion.2), channel_id=1, source_target_pairs={{0,224},{8,232},{16,240},{24,248},{32,0},{40,8},{48,16},{56,24},{6... | collective-permute-start | bytes 6291464 | tf_op jit(solution)/shard_map/ppermute | solution.py:13
  430.0 79.9 %collective-permute-start.5 = (f32[8,256,256]{2,1,0:T(8,128)}, f32[8,256,256]{2,1,0:T(8,128)S(1)}, u32[]{:S(2)}, u32[]{:S(2)}) collective-permute-start(f32[8,256,256]{2,1,0:T(8,128)} %gather_fusion.3), channel_id=1, source_target_pairs={{0,192},{8,200},{16,208},{24,216},{32,224},{40,232},{48,240},{56,2... | collective-permute-start | bytes 6291464 | tf_op jit(solution)/shard_map/ppermute | solution.py:13
  432.8 19.7 %collective-permute-start.1 = (bf16[256,1792]{1,0:T(8,128)(2,1)}, bf16[256,1792]{1,0:T(8,128)(2,1)}, u32[]{:S(2)}, u32[]{:S(2)}) collective-permute-start(bf16[256,1792]{1,0:T(8,128)(2,1)} %copy-done.2), channel_id=1, source_target_pairs={{0,8},{8,16},{16,24},{24,32},{32,40},{40,48},{48,56},{56,64},{64,7... | collective-permute-start | bytes 2752520 | tf_op jit(solution)/shard_map/ppermute | solution.py:13
  (3 other events, 5.3 us)
Sparse Core Ops, SparseCore 0:
  539.0 190.5 reduce-scatter.1
where the time goes:
time: 741 us; the launch traced here: 739 us
  waiting for transfers between devices  594 us (80%)
  local copies, waits for them, and re-layouts  77.1 us (10%)
  starting transfers between devices  31.4 us (4%)
  matrix products  19.6 us (3%)
  between operations  13.5 us (2%)
    ppermute x20, waiting for transfers between devices, from_behind(): return lax.ppermute(value, axis, pairs)  403 us
    reduce_scatter x1, waiting for transfers between devices, per_device(): summed = lax.psum_scatter(whole, 'col', scatter_dimension=0, tiled=True)  191 us
    ppermute x20, starting transfers between devices, from_behind(): return lax.ppermute(value, axis, pairs)  31.4 us
    dynamic_update_slice x15, local copies, waits for them, and re-layouts, put(): lax.dynamic_update_slice(acc, mirrors[dist - 1], (jnp.int32(0), start))  25.4 us
    dot_general x17, matrix products, product(): lax.dot_general(gradient, visiting, (((1,), (1,)), ((), ())), preferred_e...  19.6 us
    gather x4, local copies, waits for them, and re-layouts, return_tiles(): moved = from_behind(mirrors[picked], 'row', -(1 << bit))  16.6 us
  transfers between devices with their start and end apart: 21, of which 21 were waited for; matrix products, arithmetic and copies ran while one was open for 0% of the time, Pallas kernels for 0%

commit v1 on v0

v1 whole, which is shorter than its diff:
```python
import jax
import jax.numpy as jnp
import numpy as np
from jax import lax
from jax.experimental import pallas as pl
from jax.experimental.pallas import tpu as pltpu
from jax.sharding import PartitionSpec as P

NCOL = 14336
NZ = 8
AXES = ("row", "col")


def shift(value, dz=0, dy=0, dc=0):
    pairs = []
    for z in range(NZ):
        for y in range(2):
            for c in range(2):
                pairs.append(((z * 2 + y) * 2 + c, ((z + dz) % NZ * 2 + (y ^ dy)) * 2 + (c ^ dc)))
    return lax.ppermute(value, "row", pairs)


def product(left, right):
    return lax.dot_general(left, right, (((1,), (1,)), ((), ())), preferred_element_type=jnp.float32)


def arrange_kernel(where_ref, near_ref, far_ref, out_ref):
    width = out_ref.shape[1] // 32
    for block in range(32):
        place = where_ref[block]

        @pl.when(place < 20)
        def _():
            out_ref[:, block * width : (block + 1) * width] = near_ref[place] * (1.0 / NCOL)

        @pl.when(place >= 20)
        def _():
            out_ref[:, block * width : (block + 1) * width] = far_ref[place - 20] * (1.0 / NCOL)


def arrange(near, far, myself):
    z, mine = myself // 4, myself % 4
    block = jnp.arange(32)
    rel = (block % 4) ^ mine
    start = jnp.where(rel >= 2, 4, 0)
    at = (block // 4 - z - start) % 8
    where = jnp.where(at < 5, rel * 5 + at, 20 + rel * 3 + at - 5).astype(jnp.int32)
    rows, width = near.shape[1:]
    return pl.pallas_call(
        arrange_kernel,
        grid_spec=pltpu.PrefetchScalarGridSpec(
            num_scalar_prefetch=1,
            grid=(),
            in_specs=[pl.BlockSpec(memory_space=pltpu.VMEM)] * 2,
            out_specs=pl.BlockSpec(memory_space=pltpu.VMEM),
        ),
        out_shape=jax.ShapeDtypeStruct((rows, 32 * width), jnp.float32),
        compiler_params=pltpu.CompilerParams(vmem_limit_bytes=16 << 20),
    )(where, near, far)


def per_device(gradient):
    rows = gradient.shape[0]
    ncol = lax.axis_size("col")
    part = rows // ncol
    myself = lax.axis_index("row")

    above, below = shift(gradient, dz=-1), shift(gradient, dz=1)
    above, below = lax.optimization_barrier((above, below))
    above2, below2 = shift(above, dz=-1), shift(below, dz=1)
    above2, below2 = lax.optimization_barrier((above2, below2))
    other_y = shift(above2, dy=1)
    other_c = shift(below2, dc=1)
    other_x = shift(other_y, dc=1)

    window = jnp.concatenate([below2, below, gradient, above, above2], axis=0)
    sums = []
    for block in (below2, other_c, other_y, other_x):
        tiles = product(block, window).reshape(ncol, part, 5 * rows)
        sums.append(tiles)
    tiles = jnp.concatenate(sums, axis=2)
    tiles = lax.all_to_all(tiles, "col", 0, 0, tiled=True)
    total = tiles.sum(0).reshape(part, 4, 5, rows)

    home = [
        shift(total[:, 0], dz=-2),
        shift(total[:, 1], dz=-2, dc=1),
        shift(total[:, 2], dz=2, dy=1),
        shift(total[:, 3], dz=2, dy=1, dc=1),
    ]
    mirror = total[:, :, 1:4].reshape(part, 4, 3, ncol, part).transpose(3, 4, 2, 1, 0).reshape(ncol, part, 12 * part)
    mirror = lax.all_to_all(mirror, "col", 0, 0, tiled=True)
    mirror = mirror.reshape(ncol, part, 3, 4, part).transpose(2, 3, 1, 0, 4).reshape(3, 4, part, rows)
    far = [shift(mirror[2], dz=1), mirror[1], shift(mirror[0], dz=-1)]
    far = jnp.stack(far, axis=1).reshape(12, part, rows)
    near = jnp.stack(home, axis=0).transpose(0, 2, 1, 3).reshape(20, part, rows)
    return arrange(near, far, myself)


def solution(mesh):
    return jax.shard_map(
        per_device,
        mesh=mesh,
        in_specs=(P("row", "col"),),
        out_specs=P(("row", "col"), None),
        check_vma=False,
    )
```

time: 741 us -> 213 us (0.29)
  waiting for transfers between devices: 594 us -> 148 us
  local copies, waits for them, and re-layouts: 77.1 us -> 10.9 us
  matrix products: 19.6 us -> 5.52 us
  between operations: 13.5 us -> 0.2 us
    ppermute x20 -> x13, waiting for transfers between devices: 403 us -> 73.4 us  [shift(): return lax.ppermute(value, 'row', pairs)]
    reduce_scatter x1 -> x0, waiting for transfers between devices: 191 us -> none  [per_device(): summed = lax.psum_scatter(whole, 'col', scatter_dimension=0, tiled=True)]
    all_to_all x0 -> x2, waiting for transfers between devices: none -> 74.3 us  [the longest x1 74.3 us: per_device(): tiles = lax.all_to_all(tiles, 'col', 0, 0, tiled=True)]
    dynamic_update_slice x46 -> x0, local copies, waits for them, and re-layouts: 39 us -> none  [the longest x15 25.4 us: put(): lax.dynamic_update_slice(acc, mirrors[dist - 1], (jnp.int32(0), start))]
    gather x4 -> x0, local copies, waits for them, and re-layouts: 16.6 us -> none  [return_tiles(): moved = from_behind(mirrors[picked], 'row', -(1 << bit))]
    dot_general x17 -> x4, matrix products: 19.6 us -> 5.52 us  [product(): lax.dot_general(left, right, (((1,), (1,)), ((), ())), preferred_element_...]
    scatter x4 -> x0, local copies, waits for them, and re-layouts: 14 us -> none  [return_tiles(): mirrors = mirrors.at[picked].set(moved)]
    all_to_all x0 -> x2, starting transfers between devices: none -> 9.17 us  [the longest x1 5.31 us: per_device(): tiles = lax.all_to_all(tiles, 'col', 0, 0, tiled=True)]
  transfers between devices with their start and end apart: 21 -> 15, of which waited for: 21 -> 9; matrix products, arithmetic and copies ran while one was open for 0% -> 5% of each run, Pallas kernels for 0% -> 0%
where the time goes in v1:
time: 213 us; the launch traced here: 209 us
  waiting for transfers between devices  148 us (69%)
  starting transfers between devices  35.9 us (17%)
  local copies, waits for them, and re-layouts  10.9 us (5%)
  other arithmetic  6.72 us (3%)
  matrix products  5.52 us (3%)
    all_to_all x1, waiting for transfers between devices, per_device(): tiles = lax.all_to_all(tiles, 'col', 0, 0, tiled=True)  74.3 us
    ppermute x13, waiting for transfers between devices, shift(): return lax.ppermute(value, 'row', pairs)  73.4 us
    ppermute x13, starting transfers between devices, shift(): return lax.ppermute(value, 'row', pairs)  26.7 us
    dot_general x4, matrix products, product(): lax.dot_general(left, right, (((1,), (1,)), ((), ())), preferred_element_...  5.52 us
    all_to_all x1, starting transfers between devices, per_device(): tiles = lax.all_to_all(tiles, 'col', 0, 0, tiled=True)  5.31 us
  transfers between devices with their start and end apart: 15, of which 9 were waited for; matrix products, arithmetic and copies ran while one was open for 5% of the time, Pallas kernels for 0%

profile of v1, /device:TPU:32, one launch (start us, length us, event | category | flops | bytes accessed | tf_op | source)
XLA Modules:
  0.0 208.9 jit_solution(12231967641366782006)
XLA Ops:
  0.0 1.8 collective-permute-start
  2.0 20.4 %collective-permute-done = bf16[256,1792]{1,0:T(8,128)(2,1)S(1)} collective-permute-done((bf16[256,1792]{1,0:T(8,128)(2,1)}, bf16[256,1792]{1,0:T(8,128)(2,1)S(1)}, u32[]{:S(2)}, u32[]{:S(2)}) %collective-permute-start) | collective-permute-done | bytes 917536 | tf_op jit(solution)/shard_map/ppermute | solution.py:20
  22.5 3.8 %collective-permute-done.1 = bf16[256,1792]{1,0:T(8,128)(2,1)S(1)} collective-permute-done((bf16[256,1792]{1,0:T(8,128)(2,1)}, bf16[256,1792]{1,0:T(8,128)(2,1)S(1)}, u32[]{:S(2)}, u32[]{:S(2)}) %collective-permute-start.1) | collective-permute-done | bytes 917536 | tf_op jit(solution)/shard_map/ppermute | solution.py:20
  26.3 2.9 %collective-permute-start.2 = (bf16[256,1792]{1,0:T(8,128)(2,1)S(1)}, bf16[256,1792]{1,0:T(8,128)(2,1)S(1)}, u32[]{:S(2)}, u32[]{:S(2)}) collective-permute-start(bf16[256,1792]{1,0:T(8,128)(2,1)S(1)} %collective-permute-done), channel_id=1, source_target_pairs={{0,224},{8,232},{16,240},{24,248},{32,0},{40,8},{48,16},{56,24},{6... | collective-permute-start | bytes 2752520 | tf_op jit(solution)/shard_map/ppermute | solution.py:20
  29.2 18.4 %collective-permute-done.2 = bf16[256,1792]{1,0:T(8,128)(2,1)S(1)} collective-permute-done((bf16[256,1792]{1,0:T(8,128)(2,1)S(1)}, bf16[256,1792]{1,0:T(8,128)(2,1)S(1)}, u32[]{:S(2)}, u32[]{:S(2)}) %collective-permute-start.2) | collective-permute-done | bytes 917536 | tf_op jit(solution)/shard_map/ppermute | solution.py:20
  47.6 2.2 %collective-permute-done.3 = bf16[256,1792]{1,0:T(8,128)(2,1)S(1)} collective-permute-done((bf16[256,1792]{1,0:T(8,128)(2,1)S(1)}, bf16[256,1792]{1,0:T(8,128)(2,1)S(1)}, u32[]{:S(2)}, u32[]{:S(2)}) %collective-permute-start.3) | collective-permute-done | bytes 917536 | tf_op jit(solution)/shard_map/ppermute | solution.py:20
  50.0 3.3 %collective-permute-start.5 = (bf16[256,1792]{1,0:T(8,128)(2,1)S(1)}, bf16[256,1792]{1,0:T(8,128)(2,1)S(1)}, u32[]{:S(2)}, u32[]{:S(2)}) collective-permute-start(bf16[256,1792]{1,0:T(8,128)(2,1)S(1)} %collective-permute-done.2), channel_id=1, source_target_pairs={{0,16},{8,24},{16,0},{24,8},{32,48},{40,56},{48,32},{56,40},{64,80... | collective-permute-start | bytes 2752520 | tf_op jit(solution)/shard_map/ppermute | solution.py:20
  54.7 19.5 %collective-permute-done.5 = bf16[256,1792]{1,0:T(8,128)(2,1)S(1)} collective-permute-done((bf16[256,1792]{1,0:T(8,128)(2,1)S(1)}, bf16[256,1792]{1,0:T(8,128)(2,1)S(1)}, u32[]{:S(2)}, u32[]{:S(2)}) %collective-permute-start.5) | collective-permute-done | bytes 917536 | tf_op jit(solution)/shard_map/ppermute | solution.py:20
  74.3 1.4 fusion.5
  75.7 1.4 fusion.7
  77.0 1.4 fusion.6
  79.8 2.6 %pad_maximum_fusion = f32[8,32,5120]{2,1,0:T(8,128)} fusion(f32[8,32,1280]{2,1,0:T(8,128)S(1)} %bitcast.55, f32[8,32,1280]{2,1,0:T(8,128)S(1)} %bitcast.53, f32[8,32,1280]{2,1,0:T(8,128)S(1)} %bitcast.54, f32[8,32,1280]{2,1,0:T(8,128)S(1)} %bitcast.52), kind=kLoop, calls=%fused_computation | loop fusion | flops 3932160 | bytes 10485760 | tf_op jit(solution)/shard_map/concatenate | solution.py:81
  82.5 5.3 %all-to-all-start = ((f32[8,32,5120]{2,1,0:T(8,128)}), f32[8,32,5120]{2,1,0:T(8,128)}, u32[]{:S(2)}, u32[]{:S(2)}) async-start(f32[8,32,5120]{2,1,0:T(8,128)} %pad_maximum_fusion), calls=%async_computation | async-start | bytes 10485760 | tf_op jit(solution)/shard_map/all_to_all | solution.py:82
  87.8 74.3 %all-to-all-done = f32[8,32,5120]{2,1,0:T(8,128)} async-done(((f32[8,32,5120]{2,1,0:T(8,128)}), f32[8,32,5120]{2,1,0:T(8,128)}, u32[]{:S(2)}, u32[]{:S(2)}) %all-to-all-start) | async-done | bytes 5242912 | tf_op jit(solution)/shard_map/all_to_all | solution.py:82
  162.1 2.8 %reduce_sum.9 = f32[32,5120]{1,0:T(8,128)S(1)} reduce(f32[8,32,5120]{2,1,0:T(8,128)} %all-to-all-done, f32[]{:T(128)} %constant.73.clone.1), dimensions={0}, to_apply=%region_0.0 | reduce | flops 1146880 | bytes 5898244 | tf_op jit(solution)/shard_map/reduce_sum | solution.py:83
  166.0 1.8 copy.12
  167.8 2.9 %reshape.44 = f32[8,32,384]{2,1,0:T(8,128)} reshape(f32[8,32,3,4,32]{4,3,2,1,0:T(4,128)} %copy.12) | data formatting | bytes 786432 | tf_op jit(solution)/shard_map/reshape | solution.py:91
  170.7 3.9 %all-to-all-start.1 = ((f32[8,32,384]{2,1,0:T(8,128)}), f32[8,32,384]{2,1,0:T(8,128)S(1)}, u32[]{:S(2)}, u32[]{:S(2)}) async-start(f32[8,32,384]{2,1,0:T(8,128)} %reshape.44), calls=%async_computation.1 | async-start | bytes 786432 | tf_op jit(solution)/shard_map/all_to_all | solution.py:92
  176.3 4.4 %collective-permute-start.7 = (f32[32,5,256]{2,1,0:T(8,128)}, f32[32,5,256]{2,1,0:T(8,128)}, u32[]{:S(2)}, u32[]{:S(2)}) collective-permute-start(f32[32,5,256]{2,1,0:T(8,128)} %get-tuple-element.16), channel_id=1, source_target_pairs={{0,192},{8,200},{16,208},{24,216},{32,224},{40,232},{48,240},{56,2... | collective-permute-start | bytes 491528 | tf_op jit(solution)/shard_map/ppermute | solution.py:20
  181.7 2.7 %collective-permute-start.9 = (f32[32,5,256]{2,1,0:T(8,128)S(1)}, f32[32,5,256]{2,1,0:T(8,128)}, u32[]{:S(2)}, u32[]{:S(2)}) collective-permute-start(f32[32,5,256]{2,1,0:T(8,128)S(1)} %get-tuple-element.19), channel_id=1, source_target_pairs={{0,80},{8,88},{16,64},{24,72},{32,112},{40,120},{48,96},{56,104},{... | collective-permute-start | bytes 491528 | tf_op jit(solution)/shard_map/ppermute | solution.py:20
  186.8 4.4 %collective-permute-done.10 = f32[32,5,256]{2,1,0:T(8,128)S(1)} collective-permute-done((f32[32,5,256]{2,1,0:T(8,128)}, f32[32,5,256]{2,1,0:T(8,128)S(1)}, u32[]{:S(2)}, u32[]{:S(2)}) %collective-permute-start.10) | collective-permute-done | bytes 163872 | tf_op jit(solution)/shard_map/ppermute | solution.py:20
  191.3 9.1 %collective-permute-start.12 = (f32[4,32,256]{2,1,0:T(8,128)S(1)}, f32[4,32,256]{2,1,0:T(8,128)S(1)}, u32[]{:S(2)}, u32[]{:S(2)}) collective-permute-start(f32[4,32,256]{2,1,0:T(8,128)S(1)} %squeeze.23), channel_id=1, source_target_pairs={{0,224},{8,232},{16,240},{24,248},{32,0},{40,8},{48,16},{56,24},{6... | collective-permute-start | bytes 393224 | tf_op jit(solution)/shard_map/ppermute | solution.py:20
  200.4 3.7 %collective-permute-done.8 = f32[32,5,256]{2,1,0:T(8,128)} collective-permute-done((f32[32,5,256]{2,1,0:T(8,128)S(1)}, f32[32,5,256]{2,1,0:T(8,128)}, u32[]{:S(2)}, u32[]{:S(2)}) %collective-permute-start.8) | collective-permute-done | bytes 163872 | tf_op jit(solution)/shard_map/ppermute | solution.py:20
  207.0 2.0 shard_map.17
  (38 shorter events, 12.3 us)
Async XLA Ops:
  0.0 22.5 %collective-permute-start = (bf16[256,1792]{1,0:T(8,128)(2,1)}, bf16[256,1792]{1,0:T(8,128)(2,1)S(1)}, u32[]{:S(2)}, u32[]{:S(2)}) collective-permute-start(bf16[256,1792]{1,0:T(8,128)(2,1)} %param.1), channel_id=1, source_target_pairs={{0,224},{8,232},{16,240},{24,248},{32,0},{40,8},{48,16},{56,24},{6... | collective-permute-start | bytes 2752520 | tf_op jit(solution)/shard_map/ppermute | solution.py:20
  1.8 24.4 %collective-permute-start.1 = (bf16[256,1792]{1,0:T(8,128)(2,1)}, bf16[256,1792]{1,0:T(8,128)(2,1)S(1)}, u32[]{:S(2)}, u32[]{:S(2)}) collective-permute-start(bf16[256,1792]{1,0:T(8,128)(2,1)} %param.1), channel_id=1, source_target_pairs={{0,32},{8,40},{16,48},{24,56},{32,64},{40,72},{48,80},{56,88},{64,... | collective-permute-start | bytes 2752520 | tf_op jit(solution)/shard_map/ppermute | solution.py:20
  26.3 21.3 %collective-permute-start.2 = (bf16[256,1792]{1,0:T(8,128)(2,1)S(1)}, bf16[256,1792]{1,0:T(8,128)(2,1)S(1)}, u32[]{:S(2)}, u32[]{:S(2)}) collective-permute-start(bf16[256,1792]{1,0:T(8,128)(2,1)S(1)} %collective-permute-done), channel_id=1, source_target_pairs={{0,224},{8,232},{16,240},{24,248},{32,0},{40,8},{48,16},{56,24},{6... | collective-permute-start | bytes 2752520 | tf_op jit(solution)/shard_map/ppermute | solution.py:20
  29.2 20.6 %collective-permute-start.3 = (bf16[256,1792]{1,0:T(8,128)(2,1)S(1)}, bf16[256,1792]{1,0:T(8,128)(2,1)S(1)}, u32[]{:S(2)}, u32[]{:S(2)}) collective-permute-start(bf16[256,1792]{1,0:T(8,128)(2,1)S(1)} %collective-permute-done.1), channel_id=1, source_target_pairs={{0,32},{8,40},{16,48},{24,56},{32,64},{40,72},{48,80},{56,88},{64,... | collective-permute-start | bytes 2752520 | tf_op jit(solution)/shard_map/ppermute | solution.py:20
  49.9 27.2 %collective-permute-start.4 = (bf16[256,1792]{1,0:T(8,128)(2,1)S(1)}, bf16[256,1792]{1,0:T(8,128)(2,1)S(1)}, u32[]{:S(2)}, u32[]{:S(2)}) collective-permute-start(bf16[256,1792]{1,0:T(8,128)(2,1)S(1)} %collective-permute-done.3), channel_id=1, source_target_pairs={{0,8},{8,0},{16,24},{24,16},{32,40},{40,32},{48,56},{56,48},{64,72... | collective-permute-start | bytes 2752520 | tf_op jit(solution)/shard_map/ppermute | solution.py:20
  50.0 24.3 %collective-permute-start.5 = (bf16[256,1792]{1,0:T(8,128)(2,1)S(1)}, bf16[256,1792]{1,0:T(8,128)(2,1)S(1)}, u32[]{:S(2)}, u32[]{:S(2)}) collective-permute-start(bf16[256,1792]{1,0:T(8,128)(2,1)S(1)} %collective-permute-done.2), channel_id=1, source_target_pairs={{0,16},{8,24},{16,0},{24,8},{32,48},{40,56},{48,32},{56,40},{64,80... | collective-permute-start | bytes 2752520 | tf_op jit(solution)/shard_map/ppermute | solution.py:20
  74.3 4.2 %collective-permute-start.6 = (bf16[256,1792]{1,0:T(8,128)(2,1)S(1)}, bf16[256,1792]{1,0:T(8,128)(2,1)S(1)}, u32[]{:S(2)}, u32[]{:S(2)}) collective-permute-start(bf16[256,1792]{1,0:T(8,128)(2,1)S(1)} %collective-permute-done.5), channel_id=1, source_target_pairs={{0,8},{8,0},{16,24},{24,16},{32,40},{40,32},{48,56},{56,48},{64,72... | collective-permute-start | bytes 2752520 | tf_op jit(solution)/shard_map/ppermute | solution.py:20
  82.5 79.6 %all-to-all-start = ((f32[8,32,5120]{2,1,0:T(8,128)}), f32[8,32,5120]{2,1,0:T(8,128)}, u32[]{:S(2)}, u32[]{:S(2)}) async-start(f32[8,32,5120]{2,1,0:T(8,128)} %pad_maximum_fusion), calls=%async_computation | async-start | bytes 10485760 | tf_op jit(solution)/shard_map/all_to_all | solution.py:82
  170.7 13.6 %all-to-all-start.1 = ((f32[8,32,384]{2,1,0:T(8,128)}), f32[8,32,384]{2,1,0:T(8,128)S(1)}, u32[]{:S(2)}, u32[]{:S(2)}) async-start(f32[8,32,384]{2,1,0:T(8,128)} %reshape.44), calls=%async_computation.1 | async-start | bytes 786432 | tf_op jit(solution)/shard_map/all_to_all | solution.py:92
  175.5 15.8 %collective-permute-start.10 = (f32[32,5,256]{2,1,0:T(8,128)}, f32[32,5,256]{2,1,0:T(8,128)S(1)}, u32[]{:S(2)}, u32[]{:S(2)}) collective-permute-start(f32[32,5,256]{2,1,0:T(8,128)} %get-tuple-element.18), channel_id=1, source_target_pairs={{0,88},{8,80},{16,72},{24,64},{32,120},{40,112},{48,104},{56,96},{... | collective-permute-start | bytes 491528 | tf_op jit(solution)/shard_map/ppermute | solution.py:20
  176.3 24.0 %collective-permute-start.7 = (f32[32,5,256]{2,1,0:T(8,128)}, f32[32,5,256]{2,1,0:T(8,128)}, u32[]{:S(2)}, u32[]{:S(2)}) collective-permute-start(f32[32,5,256]{2,1,0:T(8,128)} %get-tuple-element.16), channel_id=1, source_target_pairs={{0,192},{8,200},{16,208},{24,216},{32,224},{40,232},{48,240},{56,2... | collective-permute-start | bytes 491528 | tf_op jit(solution)/shard_map/ppermute | solution.py:20
  180.7 23.4 %collective-permute-start.8 = (f32[32,5,256]{2,1,0:T(8,128)S(1)}, f32[32,5,256]{2,1,0:T(8,128)}, u32[]{:S(2)}, u32[]{:S(2)}) collective-permute-start(f32[32,5,256]{2,1,0:T(8,128)S(1)} %get-tuple-element.17), channel_id=1, source_target_pairs={{0,200},{8,192},{16,216},{24,208},{32,232},{40,224},{48,248},{56,2... | collective-permute-start | bytes 491528 | tf_op jit(solution)/shard_map/ppermute | solution.py:20
  181.7 22.4 %collective-permute-start.9 = (f32[32,5,256]{2,1,0:T(8,128)S(1)}, f32[32,5,256]{2,1,0:T(8,128)}, u32[]{:S(2)}, u32[]{:S(2)}) collective-permute-start(f32[32,5,256]{2,1,0:T(8,128)S(1)} %get-tuple-element.19), channel_id=1, source_target_pairs={{0,80},{8,88},{16,64},{24,72},{32,112},{40,120},{48,96},{56,104},{... | collective-permute-start | bytes 491528 | tf_op jit(solution)/shard_map/ppermute | solution.py:20
  185.9 20.1 %collective-permute-start.11 = (f32[4,32,256]{2,1,0:T(8,128)S(1)}, f32[4,32,256]{2,1,0:T(8,128)S(1)}, u32[]{:S(2)}, u32[]{:S(2)}) collective-permute-start(f32[4,32,256]{2,1,0:T(8,128)S(1)} %squeeze.22), channel_id=1, source_target_pairs={{0,32},{8,40},{16,48},{24,56},{32,64},{40,72},{48,80},{56,88},{64,... | collective-permute-start | bytes 393224 | tf_op jit(solution)/shard_map/ppermute | solution.py:20
  191.3 15.6 %collective-permute-start.12 = (f32[4,32,256]{2,1,0:T(8,128)S(1)}, f32[4,32,256]{2,1,0:T(8,128)S(1)}, u32[]{:S(2)}, u32[]{:S(2)}) collective-permute-start(f32[4,32,256]{2,1,0:T(8,128)S(1)} %squeeze.23), channel_id=1, source_target_pairs={{0,224},{8,232},{16,240},{24,248},{32,0},{40,8},{48,16},{56,24},{6... | collective-permute-start | bytes 393224 | tf_op jit(solution)/shard_map/ppermute | solution.py:20

commit v2 on v1

v2 whole, which is shorter than its diff:
```python
import jax
import jax.numpy as jnp
from jax import lax
from jax.experimental import pallas as pl
from jax.experimental.pallas import tpu as pltpu
from jax.sharding import PartitionSpec as P

NCOL = 14336
NZ = 8
LIMIT = 60000.0
LANES = 128
VMEM = pl.BlockSpec(memory_space=pltpu.VMEM)
ROOM = pltpu.CompilerParams(vmem_limit_bytes=16 << 20)


def shift(value, dz=0, dy=0, dc=0):
    pairs = []
    for z in range(NZ):
        for y in range(2):
            for c in range(2):
                pairs.append(((z * 2 + y) * 2 + c, ((z + dz) % NZ * 2 + (y ^ dy)) * 2 + (c ^ dc)))
    return lax.ppermute(value, "row", pairs)


def hold(value, *until):
    for other in until:
        corner = other[(slice(0, 1),) * other.ndim].reshape(1, 1)
        value = value + (corner * 0).astype(value.dtype)
    return value


def tiles_kernel(nrows, ncols, pairs, scaled, *refs):
    lefts, rights, out_ref = refs[:nrows], refs[nrows : nrows + ncols], refs[-1]
    ndest, part, full = out_ref.shape
    width = rights[0].shape[0]
    most = None
    for at, (left, right) in enumerate(pairs):
        tile = lax.dot_general(
            lefts[left][...], rights[right][...], (((1,), (1,)), ((), ())), preferred_element_type=jnp.float32
        )
        out_ref[:, :, at * width : (at + 1) * width] = tile.reshape(ndest, part, width)
        most = jnp.abs(tile) if most is None else jnp.maximum(most, jnp.abs(tile))
    if scaled:
        most = jnp.max(jnp.max(most, axis=0, keepdims=True), axis=1, keepdims=True)
        power = jnp.floor(jnp.log2(LIMIT / jnp.maximum(most, 1e-33)))
        factor = jnp.exp2(power) / (1.0 + lax.axis_index("col").astype(jnp.float32) / ndest)
        for at in range(len(pairs)):
            cut = slice(at * width, (at + 1) * width)
            out_ref[:, :, cut] = out_ref[:, :, cut] * factor.reshape(1, 1, 1)
        out_ref[:, :, full - LANES :] = jnp.broadcast_to(power.reshape(1, 1, 1), (ndest, part, LANES))


def tiles(lefts, rights, pairs, ndest, scaled=False):
    rows, depth = lefts[0].shape
    width = rows * len(pairs)
    return pl.pallas_call(
        lambda *refs: tiles_kernel(len(lefts), len(rights), pairs, scaled, *refs),
        in_specs=[VMEM] * (len(lefts) + len(rights)),
        out_specs=VMEM,
        out_shape=jax.ShapeDtypeStruct((ndest, rows // ndest, width + scaled * LANES), jnp.float32),
        compiler_params=ROOM,
        cost_estimate=pl.CostEstimate(
            flops=2 * rows * width * depth,
            bytes_accessed=2 * rows * depth * (len(lefts) + len(rights)) + 4 * rows * width,
            transcendentals=0,
        ),
    )(*lefts, *rights)


def turn_kernel(first_ref, second_ref, own_ref, core_ref, half_ref, cross_ref, out_ref):
    ndest, part, _ = out_ref.shape
    width = ndest * part

    def summed(ref):
        full = ref.shape[2]
        powers = [ref[source, :, full - LANES : full - LANES + 1] for source in range(ndest)]
        weights = [jnp.exp2(-power) * (1.0 + source / ndest) for source, power in enumerate(powers)]

        def total(at):
            cut = slice(at * width, (at + 1) * width)
            value = ref[0, :, cut] * weights[0]
            for source in range(1, ndest):
                value += ref[source, :, cut] * weights[source]
            return value

        return [total(at) for at in range(full // width)]

    first, second = summed(first_ref), summed(second_ref)
    for ref, blocks in (
        (own_ref, first[:3] + second[:1]),
        (core_ref, first[3:] + second[1:2]),
        (half_ref, second[2:6]),
        (cross_ref, second[6:]),
    ):
        for at, block in enumerate(blocks):
            ref[:, at * width : (at + 1) * width] = block
    groups = (
        (first[1], first[4], second[3], second[7]),
        (first[2], first[5], second[4], second[8]),
        (second[0], second[1], second[5], second[9]),
    )
    step = 4 * part
    for at, group in enumerate(groups):
        turned = jnp.concatenate(group, axis=0).T
        out_ref[:, :, at * step : (at + 1) * step] = turned.reshape(ndest, part, step)


def turn(first, second):
    ndest, part, _ = first.shape
    width = ndest * part
    bundle = jax.ShapeDtypeStruct((part, 4 * width), jnp.float32)
    return pl.pallas_call(
        turn_kernel,
        in_specs=[VMEM] * 2,
        out_specs=[VMEM] * 5,
        out_shape=[bundle] * 4 + [jax.ShapeDtypeStruct((ndest, part, 12 * part), jnp.float32)],
        compiler_params=ROOM,
    )(first, second)


def settle_kernel(in_ref, *outs):
    nsource, part, _ = in_ref.shape
    width = nsource * part
    place = 0
    for ref in outs:
        for at in range(ref.shape[1] // width):
            pieces = [in_ref[source, :, place * part : (place + 1) * part] for source in range(nsource)]
            ref[:, at * width : (at + 1) * width] = jnp.concatenate(pieces, axis=1)
            place += 1


def settle(turned):
    nsource, part, _ = turned.shape
    width = nsource * part
    return pl.pallas_call(
        settle_kernel,
        in_specs=[VMEM],
        out_specs=[VMEM] * 5,
        out_shape=[jax.ShapeDtypeStruct((part, count * width), jnp.float32) for count in (4, 2, 2, 2, 2)],
        compiler_params=ROOM,
    )(turned)


def arrange_kernel(to_ref, *refs):
    blocks, out_ref = refs[:-1], refs[-1]
    place = 0
    width = out_ref.shape[1] // 32
    for ref in blocks:
        for at in range(ref.shape[1] // width):
            start = pl.multiple_of(to_ref[place] * width, width)
            out_ref[:, pl.ds(start, width)] = ref[:, at * width : (at + 1) * width] * (1.0 / NCOL)
            place += 1


def arrange(blocks, labels, myself, rows, width):
    z, mine = myself // 4, myself % 4
    rel = jnp.array([k for k, _ in labels], jnp.int32)
    slab = jnp.array([d for _, d in labels], jnp.int32)
    to = ((z + slab) % NZ * 4 + (rel ^ mine)).astype(jnp.int32)
    return pl.pallas_call(
        arrange_kernel,
        grid_spec=pltpu.PrefetchScalarGridSpec(
            num_scalar_prefetch=1, grid=(), in_specs=[VMEM] * len(blocks), out_specs=VMEM
        ),
        out_shape=jax.ShapeDtypeStruct((rows, 32 * width), jnp.float32),
        compiler_params=ROOM,
    )(to, *blocks)


def per_device(gradient):
    rows = gradient.shape[0]
    ncol = lax.axis_size("col")
    part = rows // ncol
    myself = lax.axis_index("row")

    def exchange(parts):
        return lax.all_to_all(parts, "col", 0, 0, tiled=True)

    up1, down1 = shift(gradient, dz=-1), shift(gradient, dz=1)
    half1 = shift(up1, dy=1)
    core1 = shift(hold(down1, up1), dc=1)
    up2, down2 = shift(up1, dz=-1), shift(down1, dz=1)

    near = [(row, column) for row in range(2) for column in range(3)]
    first = tiles([down1, core1], [down1, gradient, up1], near, ncol, scaled=True)
    half1 = hold(half1, first)
    cross1 = shift(half1, dc=1)
    first = exchange(first.astype(jnp.float16))
    up3, down3 = shift(hold(up2, first), dz=-1), shift(hold(down2, first), dz=1)
    middle = [(0, 0), (1, 0)] + [(row, column) for row in (2, 3) for column in (1, 2, 3, 4)]
    second = tiles([down1, core1, half1, cross1], [up2, up1, gradient, down1, down2], middle, ncol, scaled=True)
    second = exchange(second.astype(jnp.float16))
    own, core, half, cross, turned = turn(first.astype(jnp.float32), second.astype(jnp.float32))

    last = tiles([up3, down3], [down1, core1, half1, cross1], [(0, 0), (0, 1), (1, 2), (1, 3)], ncol)
    last = exchange(jnp.concatenate([last, turned], axis=2))
    opposite, turned = last[:, :, : 4 * rows].sum(0), last[:, :, 4 * rows :]

    home = [
        shift(own, dz=-1),
        shift(core, dz=-1, dc=1),
        shift(half, dz=1, dy=1),
        shift(cross, dz=1, dy=1, dc=1),
    ]
    home_labels = [(k, d if k < 2 else -d) for k in range(4) for d in range(4)]
    still, above1, below1, above2, below2 = settle(turned)
    away = [
        still,
        shift(above1, dz=1),
        shift(below1, dz=-1),
        shift(above2, dz=2),
        shift(below2, dz=-2),
        shift(opposite[:, : 2 * rows], dz=3),
        shift(opposite[:, 2 * rows :], dz=-3),
    ]
    away_labels = [(0, -1), (1, -1), (2, 1), (3, 1), (0, -2), (1, -2), (2, 2), (3, 2), (0, -3), (1, -3), (2, 3), (3, 3)]
    away_labels += [(k, 4) for k in range(4)]
    return arrange(home + away, home_labels + away_labels, myself, part, rows)


def solution(mesh):
    return jax.shard_map(
        per_device,
        mesh=mesh,
        in_specs=(P("row", "col"),),
        out_specs=P(("row", "col"), None),
        check_vma=False,
    )
```

time: 213 us -> 164 us (0.77); the launches traced: 209 us -> 163 us
  waiting for transfers between devices: 148 us -> 80.2 us
  starting transfers between devices: 35.9 us -> 46.9 us
  Pallas kernels: 1.99 us -> 12.9 us
  other arithmetic: 6.72 us -> 13.6 us
  matrix products: 5.52 us -> 0 us
  local copies, waits for them, and re-layouts: 10.9 us -> 6.88 us
    all_to_all x2 -> x3, waiting for transfers between devices: 74.3 us -> 14.9 us  [exchange(): return lax.all_to_all(parts, 'col', 0, 0, tiled=True)]
    pallas_call x0 -> x5, Pallas kernels: none -> 11.3 us  [the longest x3 10.5 us: tiles(): pl.pallas_call(lambda *refs: tiles_kernel(len(lefts), len(rights), pairs,...]
    ppermute x13 -> x19, waiting for transfers between devices: 73.4 us -> 65.3 us  [shift(): return lax.ppermute(value, 'row', pairs)]
    convert_element_type x0 -> x4, other arithmetic: none -> 6.38 us  [the longest x1 2.5 us: per_device(): first.astype(jnp.float32)]
    all_to_all x2 -> x3, starting transfers between devices: 9.17 us -> 15.1 us  [exchange(): return lax.all_to_all(parts, 'col', 0, 0, tiled=True)]
    dot_general x4 -> x0, matrix products: 5.52 us -> none  [product(): lax.dot_general(left, right, (((1,), (1,)), ((), ())), preferred_element_...]
    ppermute x13 -> x19, starting transfers between devices: 26.7 us -> 31.7 us  [shift(): return lax.ppermute(value, 'row', pairs)]
    add x0 -> x5, other arithmetic: none -> 4.72 us  [the longest x4 4.71 us: hold(): value = value + (corner * 0).astype(value.dtype)]
  transfers between devices with their start and end apart: 15 -> 22, of which waited for: 9 -> 8; matrix products, arithmetic and copies ran while one was open for 5% -> 9% of each run, Pallas kernels for 0% -> 7%
where the time goes in v2:
time: 164 us; the launch traced here: 163 us
  waiting for transfers between devices  80.2 us (49%)
  starting transfers between devices  46.9 us (29%)
  other arithmetic  13.6 us (8%)
  Pallas kernels  12.9 us (8%)
  local copies, waits for them, and re-layouts  6.88 us (4%)
  between operations  2.22 us (1%)
    ppermute x19, waiting for transfers between devices, shift(): return lax.ppermute(value, 'row', pairs)  65.3 us
    ppermute x19, starting transfers between devices, shift(): return lax.ppermute(value, 'row', pairs)  31.7 us
    all_to_all x3, starting transfers between devices, exchange(): return lax.all_to_all(parts, 'col', 0, 0, tiled=True)  15.1 us
    all_to_all x3, waiting for transfers between devices, exchange(): return lax.all_to_all(parts, 'col', 0, 0, tiled=True)  14.9 us
    pallas_call x3, Pallas kernels, tiles(): pl.pallas_call(lambda *refs: tiles_kernel(len(lefts), len(rights), pairs,...  10.5 us
    add x4, other arithmetic, hold(): value = value + (corner * 0).astype(value.dtype)  4.71 us
  transfers between devices with their start and end apart: 22, of which 8 were waited for; matrix products, arithmetic and copies ran while one was open for 9% of the time, Pallas kernels for 7%

profile of v2, /device:TPU:32, one launch (start us, length us, event | category | flops | bytes accessed | tf_op | source)
XLA Modules:
  0.0 162.7 jit_solution(7563977795861497512)
XLA Ops:
  0.0 1.8 %collective-permute-start.1 = (bf16[256,1792]{1,0:T(8,128)(2,1)}, bf16[256,1792]{1,0:T(8,128)(2,1)}, u32[]{:S(2)}, u32[]{:S(2)}) collective-permute-start(bf16[256,1792]{1,0:T(8,128)(2,1)} %refs_6_.1), channel_id=1, source_target_pairs={{0,224},{8,232},{16,240},{24,248},{32,0},{40,8},{48,16},{56,24},{6... | collective-permute-start | bytes 2752520 | tf_op jit(solution)/shard_map/ppermute | solution.py:22
  2.0 20.6 %collective-permute-done.1.refs_4_.refs_5_ = bf16[256,1792]{1,0:T(8,128)(2,1)} collective-permute-done((bf16[256,1792]{1,0:T(8,128)(2,1)}, bf16[256,1792]{1,0:T(8,128)(2,1)}, u32[]{:S(2)}, u32[]{:S(2)}) %collective-permute-start.1) | collective-permute-done | bytes 917536 | tf_op jit(solution)/shard_map/ppermute | solution.py:22
  26.4 3.3 %collective-permute-start.3 = (bf16[256,1792]{1,0:T(8,128)(2,1)}, bf16[256,1792]{1,0:T(8,128)(2,1)S(1)}, u32[]{:S(2)}, u32[]{:S(2)}) collective-permute-start(bf16[256,1792]{1,0:T(8,128)(2,1)} %collective-permute-done.1.refs_4_.refs_5_), channel_id=1, source_target_pairs={{0,16},{8,24},{16,0},{24,8},{32,48},{40,56},{48,32},{56,40},{64,80... | collective-permute-start | bytes 2752520 | tf_op jit(solution)/shard_map/ppermute | solution.py:22
  29.7 2.9 %collective-permute-start.5 = (bf16[256,1792]{1,0:T(8,128)(2,1)}, bf16[256,1792]{1,0:T(8,128)(2,1)}, u32[]{:S(2)}, u32[]{:S(2)}) collective-permute-start(bf16[256,1792]{1,0:T(8,128)(2,1)} %collective-permute-done.1.refs_4_.refs_5_), channel_id=1, source_target_pairs={{0,224},{8,232},{16,240},{24,248},{32,0},{40,8},{48,16},{56,24},{6... | collective-permute-start | bytes 2752520 | tf_op jit(solution)/shard_map/ppermute | solution.py:22
  32.7 3.0 %shard_map.37 = f32[8,32,1664]{2,1,0:T(8,128)S(1)} custom-call(bf16[256,1792]{1,0:T(8,128)(2,1)S(1)} %collective-permute-done.refs_0_.refs_2_.refs_7_, bf16[256,1792]{1,0:T(8,128)(2,1)S(1)} %collective-permute-done.2.refs_1_.refs_3_, bf16[256,1792]{1,0:T(8,128)(2,1)S(1)} %collective-permute-done.refs_0_.refs_2_.refs_7_, bf16[256,1792]{1,0:T(8,128)(2,1)S(1)} %copy-done.3, ...), custom_call_target="tpu_custom_call" | custom-call | flops 1409286144 | bytes 6160384 | tf_op jit(solution)/shard_map/pallas_call | solution.py:56
  37.2 4.4 %all-to-all-start = ((f16[8,32,1664]{2,1,0:T(8,128)(2,1)}), f16[8,32,1664]{2,1,0:T(8,128)(2,1)}, u32[]{:S(2)}, u32[]{:S(2)}) async-start(f16[8,32,1664]{2,1,0:T(8,128)(2,1)} %convert_element_type.21), calls=%async_computation | async-start | bytes 1703936 | tf_op jit(solution)/shard_map/all_to_all | solution.py:177
  42.3 16.0 %collective-permute-done.3 = bf16[256,1792]{1,0:T(8,128)(2,1)S(1)} collective-permute-done((bf16[256,1792]{1,0:T(8,128)(2,1)}, bf16[256,1792]{1,0:T(8,128)(2,1)S(1)}, u32[]{:S(2)}, u32[]{:S(2)}) %collective-permute-start.3) | collective-permute-done | bytes 917536 | tf_op jit(solution)/shard_map/ppermute | solution.py:22
  62.5 2.2 %broadcast_add_fusion.1 = bf16[256,1792]{1,0:T(8,128)(2,1)} fusion(bf16[256,1792]{1,0:T(8,128)(2,1)} %collective-permute-done.5.refs_4_, bf16[]{:T(256)} %bitcast.2), kind=kLoop, calls=%fused_computation.3 | loop fusion | flops 458752 | bytes 1835010 | tf_op jit(solution)/shard_map/add | solution.py:28
  64.6 2.9 %collective-permute-start.11 = (bf16[256,1792]{1,0:T(8,128)(2,1)}, bf16[256,1792]{1,0:T(8,128)(2,1)}, u32[]{:S(2)}, u32[]{:S(2)}) collective-permute-start(bf16[256,1792]{1,0:T(8,128)(2,1)} %broadcast_add_fusion.1), channel_id=1, source_target_pairs={{0,224},{8,232},{16,240},{24,248},{32,0},{40,8},{48,16},{56,24},{6... | collective-permute-start | bytes 2752520 | tf_op jit(solution)/shard_map/ppermute | solution.py:22
  67.6 4.9 %shard_map.38 = f32[8,32,2688]{2,1,0:T(8,128)S(1)} custom-call(bf16[256,1792]{1,0:T(8,128)(2,1)S(1)} %collective-permute-done.refs_0_.refs_2_.refs_7_, bf16[256,1792]{1,0:T(8,128)(2,1)S(1)} %collective-permute-done.2.refs_1_.refs_3_, bf16[256,1792]{1,0:T(8,128)(2,1)S(1)} %broadcast_add_fusion.2.refs_2_.refs_4_, ...), custom_call_target="tpu_custom_call" | custom-call | flops 2348810240 | bytes 10878976 | tf_op jit(solution)/shard_map/pallas_call | solution.py:56
  73.7 5.3 %all-to-all-start.1 = ((f16[8,32,2688]{2,1,0:T(8,128)(2,1)}), f16[8,32,2688]{2,1,0:T(8,128)(2,1)}, u32[]{:S(2)}, u32[]{:S(2)}) async-start(f16[8,32,2688]{2,1,0:T(8,128)(2,1)} %convert_element_type.24), calls=%async_computation.1 | async-start | bytes 2752512 | tf_op jit(solution)/shard_map/all_to_all | solution.py:177
  80.3 2.5 %convert_element_type.22.first_ref = f32[8,32,1664]{2,1,0:T(8,128)} convert(f16[8,32,1664]{2,1,0:T(8,128)(2,1)} %all-to-all-done) | non-fusion elementwise | flops 425984 | bytes 2555904 | tf_op jit(solution)/shard_map/convert_element_type | solution.py:193
  82.8 5.3 %collective-permute-done.11.refs_0_ = bf16[256,1792]{1,0:T(8,128)(2,1)} collective-permute-done((bf16[256,1792]{1,0:T(8,128)(2,1)}, bf16[256,1792]{1,0:T(8,128)(2,1)}, u32[]{:S(2)}, u32[]{:S(2)}) %collective-permute-start.11) | collective-permute-done | bytes 917536 | tf_op jit(solution)/shard_map/ppermute | solution.py:22
  88.1 14.8 %collective-permute-done.12.refs_1_ = bf16[256,1792]{1,0:T(8,128)(2,1)S(1)} collective-permute-done((bf16[256,1792]{1,0:T(8,128)(2,1)S(1)}, bf16[256,1792]{1,0:T(8,128)(2,1)S(1)}, u32[]{:S(2)}, u32[]{:S(2)}) %collective-permute-start.12) | collective-permute-done | bytes 917536 | tf_op jit(solution)/shard_map/ppermute | solution.py:22
  103.0 2.6 %shard_map.40 = f32[8,32,1024]{2,1,0:T(8,128)S(1)} custom-call(bf16[256,1792]{1,0:T(8,128)(2,1)} %collective-permute-done.11.refs_0_, bf16[256,1792]{1,0:T(8,128)(2,1)S(1)} %collective-permute-done.12.refs_1_, bf16[256,1792]{1,0:T(8,128)(2,1)S(1)} %collective-permute-done.refs_0_.refs_2_.refs_7_, ...), custom_call_target="tpu_custom_call" | custom-call | flops 939524096 | bytes 6553600 | tf_op jit(solution)/shard_map/pallas_call | solution.py:56
  110.9 5.4 %all-to-all-start.2 = ((f32[8,32,1408]{2,1,0:T(8,128)}), f32[8,32,1408]{2,1,0:T(8,128)}, u32[]{:S(2)}, u32[]{:S(2)}) async-start(f32[8,32,1408]{2,1,0:T(8,128)} %pad_maximum_fusion), calls=%async_computation.2 | async-start | bytes 2883584 | tf_op jit(solution)/shard_map/all_to_all | solution.py:177
  116.9 2.5 %collective-permute-start.7 = (f32[32,1024]{1,0:T(8,128)S(1)}, f32[32,1024]{1,0:T(8,128)S(1)}, u32[]{:S(2)}, u32[]{:S(2)}) collective-permute-start(f32[32,1024]{1,0:T(8,128)S(1)} %get-tuple-element.15), channel_id=1, source_target_pairs={{0,224},{8,232},{16,240},{24,248},{32,0},{40,8},{48,16},{56,24},{6... | collective-permute-start | bytes 393224 | tf_op jit(solution)/shard_map/ppermute | solution.py:22
  119.4 4.9 %collective-permute-start.8 = (f32[32,1024]{1,0:T(8,128)S(1)}, f32[32,1024]{1,0:T(8,128)S(1)}, u32[]{:S(2)}, u32[]{:S(2)}) collective-permute-start(f32[32,1024]{1,0:T(8,128)S(1)} %get-tuple-element.16), channel_id=1, source_target_pairs={{0,232},{8,224},{16,248},{24,240},{32,8},{40,0},{48,24},{56,16},{6... | collective-permute-start | bytes 393224 | tf_op jit(solution)/shard_map/ppermute | solution.py:22
  124.4 14.9 %all-to-all-done.2 = f32[8,32,1408]{2,1,0:T(8,128)} async-done(((f32[8,32,1408]{2,1,0:T(8,128)}), f32[8,32,1408]{2,1,0:T(8,128)}, u32[]{:S(2)}, u32[]{:S(2)}) %all-to-all-start.2) | async-done | bytes 1441824 | tf_op jit(solution)/shard_map/all_to_all | solution.py:177
  142.1 3.0 %collective-permute-start.14 = (f32[32,512]{1,0:T(8,128)S(1)}, f32[32,512]{1,0:T(8,128)S(1)}, u32[]{:S(2)}, u32[]{:S(2)}) collective-permute-start(f32[32,512]{1,0:T(8,128)S(1)} %get-tuple-element.22), channel_id=1, source_target_pairs={{0,224},{8,232},{16,240},{24,248},{32,0},{40,8},{48,16},{56,24},{6... | collective-permute-start | bytes 196616 | tf_op jit(solution)/shard_map/ppermute | solution.py:22
  146.0 3.3 %collective-permute-start.16 = (f32[32,512]{1,0:T(8,128)S(1)}, f32[32,512]{1,0:T(8,128)S(1)}, u32[]{:S(2)}, u32[]{:S(2)}) collective-permute-start(f32[32,512]{1,0:T(8,128)S(1)} %get-tuple-element.24), channel_id=1, source_target_pairs={{0,192},{8,200},{16,208},{24,216},{32,224},{40,232},{48,240},{56,2... | collective-permute-start | bytes 196616 | tf_op jit(solution)/shard_map/ppermute | solution.py:22
  149.3 3.4 %collective-permute-start.17 = (f32[32,512]{1,0:T(8,128)S(1)}, f32[32,512]{1,0:T(8,128)S(1)}, u32[]{:S(2)}, u32[]{:S(2)}) collective-permute-start(f32[32,512]{1,0:T(8,128)S(1)} %get-tuple-element.26), channel_id=1, source_target_pairs={{0,96},{8,104},{16,112},{24,120},{32,128},{40,136},{48,144},{56,15... | collective-permute-start | bytes 196616 | tf_op jit(solution)/shard_map/ppermute | solution.py:22
  154.4 2.7 %collective-permute-done.17.refs_9_ = f32[32,512]{1,0:T(8,128)S(1)} collective-permute-done((f32[32,512]{1,0:T(8,128)S(1)}, f32[32,512]{1,0:T(8,128)S(1)}, u32[]{:S(2)}, u32[]{:S(2)}) %collective-permute-start.17) | collective-permute-done | bytes 65568 | tf_op jit(solution)/shard_map/ppermute | solution.py:22
  157.0 4.1 %collective-permute-done.18.refs_10_ = f32[32,512]{1,0:T(8,128)S(1)} collective-permute-done((f32[32,512]{1,0:T(8,128)S(1)}, f32[32,512]{1,0:T(8,128)S(1)}, u32[]{:S(2)}, u32[]{:S(2)}) %collective-permute-start.18) | collective-permute-done | bytes 65568 | tf_op jit(solution)/shard_map/ppermute | solution.py:22
  (58 shorter events, 23.7 us)
Async XLA Ops:
  0.0 22.7 %collective-permute-start.1 = (bf16[256,1792]{1,0:T(8,128)(2,1)}, bf16[256,1792]{1,0:T(8,128)(2,1)}, u32[]{:S(2)}, u32[]{:S(2)}) collective-permute-start(bf16[256,1792]{1,0:T(8,128)(2,1)} %refs_6_.1), channel_id=1, source_target_pairs={{0,224},{8,232},{16,240},{24,248},{32,0},{40,8},{48,16},{56,24},{6... | collective-permute-start | bytes 2752520 | tf_op jit(solution)/shard_map/ppermute | solution.py:22
  1.8 24.4 %collective-permute-start = (bf16[256,1792]{1,0:T(8,128)(2,1)}, bf16[256,1792]{1,0:T(8,128)(2,1)S(1)}, u32[]{:S(2)}, u32[]{:S(2)}) collective-permute-start(bf16[256,1792]{1,0:T(8,128)(2,1)} %refs_6_.1), channel_id=1, source_target_pairs={{0,32},{8,40},{16,48},{24,56},{32,64},{40,72},{48,80},{56,88},{64,... | collective-permute-start | bytes 2752520 | tf_op jit(solution)/shard_map/ppermute | solution.py:22
  26.3 6.3 %collective-permute-start.2 = (bf16[256,1792]{1,0:T(8,128)(2,1)S(1)}, bf16[256,1792]{1,0:T(8,128)(2,1)S(1)}, u32[]{:S(2)}, u32[]{:S(2)}) collective-permute-start(bf16[256,1792]{1,0:T(8,128)(2,1)S(1)} %broadcast_add_fusion.3), channel_id=1, source_target_pairs={{0,8},{8,0},{16,24},{24,16},{32,40},{40,32},{48,56},{56,48},{64,72... | collective-permute-start | bytes 2752520 | tf_op jit(solution)/shard_map/ppermute | solution.py:22
  26.4 31.8 %collective-permute-start.3 = (bf16[256,1792]{1,0:T(8,128)(2,1)}, bf16[256,1792]{1,0:T(8,128)(2,1)S(1)}, u32[]{:S(2)}, u32[]{:S(2)}) collective-permute-start(bf16[256,1792]{1,0:T(8,128)(2,1)} %collective-permute-done.1.refs_4_.refs_5_), channel_id=1, source_target_pairs={{0,16},{8,24},{16,0},{24,8},{32,48},{40,56},{48,32},{56,40},{64,80... | collective-permute-start | bytes 2752520 | tf_op jit(solution)/shard_map/ppermute | solution.py:22
  29.7 32.7 %collective-permute-start.5 = (bf16[256,1792]{1,0:T(8,128)(2,1)}, bf16[256,1792]{1,0:T(8,128)(2,1)}, u32[]{:S(2)}, u32[]{:S(2)}) collective-permute-start(bf16[256,1792]{1,0:T(8,128)(2,1)} %collective-permute-done.1.refs_4_.refs_5_), channel_id=1, source_target_pairs={{0,224},{8,232},{16,240},{24,248},{32,0},{40,8},{48,16},{56,24},{6... | collective-permute-start | bytes 2752520 | tf_op jit(solution)/shard_map/ppermute | solution.py:22
  32.6 34.9 %collective-permute-start.6 = (bf16[256,1792]{1,0:T(8,128)(2,1)S(1)}, bf16[256,1792]{1,0:T(8,128)(2,1)}, u32[]{:S(2)}, u32[]{:S(2)}) collective-permute-start(bf16[256,1792]{1,0:T(8,128)(2,1)S(1)} %collective-permute-done.refs_0_.refs_2_.refs_7_), channel_id=1, source_target_pairs={{0,32},{8,40},{16,48},{24,56},{32,64},{40,72},{48,80},{56,88},{64,... | collective-permute-start | bytes 2752520 | tf_op jit(solution)/shard_map/ppermute | solution.py:22
  37.2 23.3 %all-to-all-start = ((f16[8,32,1664]{2,1,0:T(8,128)(2,1)}), f16[8,32,1664]{2,1,0:T(8,128)(2,1)}, u32[]{:S(2)}, u32[]{:S(2)}) async-start(f16[8,32,1664]{2,1,0:T(8,128)(2,1)} %convert_element_type.21), calls=%async_computation | async-start | bytes 1703936 | tf_op jit(solution)/shard_map/all_to_all | solution.py:177
  60.4 7.2 %collective-permute-start.4 = (bf16[256,1792]{1,0:T(8,128)(2,1)S(1)}, bf16[256,1792]{1,0:T(8,128)(2,1)}, u32[]{:S(2)}, u32[]{:S(2)}) collective-permute-start(bf16[256,1792]{1,0:T(8,128)(2,1)S(1)} %broadcast_add_fusion.2.refs_2_.refs_4_), channel_id=1, source_target_pairs={{0,8},{8,0},{16,24},{24,16},{32,40},{40,32},{48,56},{56,48},{64,72... | collective-permute-start | bytes 2752520 | tf_op jit(solution)/shard_map/ppermute | solution.py:22
  64.6 23.5 %collective-permute-start.11 = (bf16[256,1792]{1,0:T(8,128)(2,1)}, bf16[256,1792]{1,0:T(8,128)(2,1)}, u32[]{:S(2)}, u32[]{:S(2)}) collective-permute-start(bf16[256,1792]{1,0:T(8,128)(2,1)} %broadcast_add_fusion.1), channel_id=1, source_target_pairs={{0,224},{8,232},{16,240},{24,248},{32,0},{40,8},{48,16},{56,24},{6... | collective-permute-start | bytes 2752520 | tf_op jit(solution)/shard_map/ppermute | solution.py:22
  73.7 32.9 %all-to-all-start.1 = ((f16[8,32,2688]{2,1,0:T(8,128)(2,1)}), f16[8,32,2688]{2,1,0:T(8,128)(2,1)}, u32[]{:S(2)}, u32[]{:S(2)}) async-start(f16[8,32,2688]{2,1,0:T(8,128)(2,1)} %convert_element_type.24), calls=%async_computation.1 | async-start | bytes 2752512 | tf_op jit(solution)/shard_map/all_to_all | solution.py:177
  80.2 22.7 %collective-permute-start.12 = (bf16[256,1792]{1,0:T(8,128)(2,1)S(1)}, bf16[256,1792]{1,0:T(8,128)(2,1)S(1)}, u32[]{:S(2)}, u32[]{:S(2)}) collective-permute-start(bf16[256,1792]{1,0:T(8,128)(2,1)S(1)} %broadcast_add_fusion), channel_id=1, source_target_pairs={{0,32},{8,40},{16,48},{24,56},{32,64},{40,72},{48,80},{56,88},{64,... | collective-permute-start | bytes 2752520 | tf_op jit(solution)/shard_map/ppermute | solution.py:22
  110.9 28.4 %all-to-all-start.2 = ((f32[8,32,1408]{2,1,0:T(8,128)}), f32[8,32,1408]{2,1,0:T(8,128)}, u32[]{:S(2)}, u32[]{:S(2)}) async-start(f32[8,32,1408]{2,1,0:T(8,128)} %pad_maximum_fusion), calls=%async_computation.2 | async-start | bytes 2883584 | tf_op jit(solution)/shard_map/all_to_all | solution.py:177
  116.3 38.0 %copy-start.6 = (s32[32]{0:T(128)S(1)}, s32[32]{0:T(128)}, u32[]{:S(2)}) copy-start(s32[32]{0:T(128)} %constant.61.clone) | copy-start | bytes 388
  116.3 38.0 %copy-start.7 = (s32[32]{0:T(128)S(1)}, s32[32]{0:T(128)}, u32[]{:S(2)}) copy-start(s32[32]{0:T(128)} %constant.62.clone) | copy-start | bytes 388
  116.3 25.8 %collective-permute-start.10 = (f32[32,1024]{1,0:T(8,128)S(1)}, f32[32,1024]{1,0:T(8,128)S(1)}, u32[]{:S(2)}, u32[]{:S(2)}) collective-permute-start(f32[32,1024]{1,0:T(8,128)S(1)} %get-tuple-element.18), channel_id=1, source_target_pairs={{0,56},{8,48},{16,40},{24,32},{32,88},{40,80},{48,72},{56,64},{64,... | collective-permute-start | bytes 393224 | tf_op jit(solution)/shard_map/ppermute | solution.py:22
  116.9 28.2 %collective-permute-start.7 = (f32[32,1024]{1,0:T(8,128)S(1)}, f32[32,1024]{1,0:T(8,128)S(1)}, u32[]{:S(2)}, u32[]{:S(2)}) collective-permute-start(f32[32,1024]{1,0:T(8,128)S(1)} %get-tuple-element.15), channel_id=1, source_target_pairs={{0,224},{8,232},{16,240},{24,248},{32,0},{40,8},{48,16},{56,24},{6... | collective-permute-start | bytes 393224 | tf_op jit(solution)/shard_map/ppermute | solution.py:22
  119.4 26.6 %collective-permute-start.8 = (f32[32,1024]{1,0:T(8,128)S(1)}, f32[32,1024]{1,0:T(8,128)S(1)}, u32[]{:S(2)}, u32[]{:S(2)}) collective-permute-start(f32[32,1024]{1,0:T(8,128)S(1)} %get-tuple-element.16), channel_id=1, source_target_pairs={{0,232},{8,224},{16,248},{24,240},{32,8},{40,0},{48,24},{56,16},{6... | collective-permute-start | bytes 393224 | tf_op jit(solution)/shard_map/ppermute | solution.py:22
  124.4 24.9 %collective-permute-start.9 = (f32[32,1024]{1,0:T(8,128)S(1)}, f32[32,1024]{1,0:T(8,128)S(1)}, u32[]{:S(2)}, u32[]{:S(2)}) collective-permute-start(f32[32,1024]{1,0:T(8,128)S(1)} %get-tuple-element.17), channel_id=1, source_target_pairs={{0,48},{8,56},{16,32},{24,40},{32,80},{40,88},{48,64},{56,72},{64,... | collective-permute-start | bytes 393224 | tf_op jit(solution)/shard_map/ppermute | solution.py:22
  140.7 12.0 %collective-permute-start.13 = (f32[32,512]{1,0:T(8,128)S(1)}, f32[32,512]{1,0:T(8,128)S(1)}, u32[]{:S(2)}, u32[]{:S(2)}) collective-permute-start(f32[32,512]{1,0:T(8,128)S(1)} %get-tuple-element.21), channel_id=1, source_target_pairs={{0,32},{8,40},{16,48},{24,56},{32,64},{40,72},{48,80},{56,88},{64,... | collective-permute-start | bytes 196616 | tf_op jit(solution)/shard_map/ppermute | solution.py:22
  142.1 12.2 %collective-permute-start.14 = (f32[32,512]{1,0:T(8,128)S(1)}, f32[32,512]{1,0:T(8,128)S(1)}, u32[]{:S(2)}, u32[]{:S(2)}) collective-permute-start(f32[32,512]{1,0:T(8,128)S(1)} %get-tuple-element.22), channel_id=1, source_target_pairs={{0,224},{8,232},{16,240},{24,248},{32,0},{40,8},{48,16},{56,24},{6... | collective-permute-start | bytes 196616 | tf_op jit(solution)/shard_map/ppermute | solution.py:22
  145.1 9.2 %collective-permute-start.15 = (f32[32,512]{1,0:T(8,128)S(1)}, f32[32,512]{1,0:T(8,128)S(1)}, u32[]{:S(2)}, u32[]{:S(2)}) collective-permute-start(f32[32,512]{1,0:T(8,128)S(1)} %get-tuple-element.23), channel_id=1, source_target_pairs={{0,64},{8,72},{16,80},{24,88},{32,96},{40,104},{48,112},{56,120},{... | collective-permute-start | bytes 196616 | tf_op jit(solution)/shard_map/ppermute | solution.py:22
  146.0 8.3 %collective-permute-start.16 = (f32[32,512]{1,0:T(8,128)S(1)}, f32[32,512]{1,0:T(8,128)S(1)}, u32[]{:S(2)}, u32[]{:S(2)}) collective-permute-start(f32[32,512]{1,0:T(8,128)S(1)} %get-tuple-element.24), channel_id=1, source_target_pairs={{0,192},{8,200},{16,208},{24,216},{32,224},{40,232},{48,240},{56,2... | collective-permute-start | bytes 196616 | tf_op jit(solution)/shard_map/ppermute | solution.py:22
  149.3 7.7 %collective-permute-start.17 = (f32[32,512]{1,0:T(8,128)S(1)}, f32[32,512]{1,0:T(8,128)S(1)}, u32[]{:S(2)}, u32[]{:S(2)}) collective-permute-start(f32[32,512]{1,0:T(8,128)S(1)} %get-tuple-element.26), channel_id=1, source_target_pairs={{0,96},{8,104},{16,112},{24,120},{32,128},{40,136},{48,144},{56,15... | collective-permute-start | bytes 196616 | tf_op jit(solution)/shard_map/ppermute | solution.py:22
  152.7 8.4 %collective-permute-start.18 = (f32[32,512]{1,0:T(8,128)S(1)}, f32[32,512]{1,0:T(8,128)S(1)}, u32[]{:S(2)}, u32[]{:S(2)}) collective-permute-start(f32[32,512]{1,0:T(8,128)S(1)} %get-tuple-element.25), channel_id=1, source_target_pairs={{0,160},{8,168},{16,176},{24,184},{32,192},{40,200},{48,208},{56,2... | collective-permute-start | bytes 196616 | tf_op jit(solution)/shard_map/ppermute | solution.py:22
  (6 other events, 44.7 us)

commit v3 on v2

--- a/solution.py
+++ b/solution.py
@@ -9,8 +9,9 @@
 NZ = 8
 LIMIT = 60000.0
 LANES = 128
+SPLIT = 8193.0
 VMEM = pl.BlockSpec(memory_space=pltpu.VMEM)
-ROOM = pltpu.CompilerParams(vmem_limit_bytes=16 << 20)
+ROOM = pltpu.CompilerParams(vmem_limit_bytes=14 << 20)
 
 
 def shift(value, dz=0, dy=0, dc=0):
@@ -42,7 +43,7 @@
         most = jnp.abs(tile) if most is None else jnp.maximum(most, jnp.abs(tile))
     if scaled:
         most = jnp.max(jnp.max(most, axis=0, keepdims=True), axis=1, keepdims=True)
-        power = jnp.floor(jnp.log2(LIMIT / jnp.maximum(most, 1e-33)))
+        power = power_of(most)
         factor = jnp.exp2(power) / (1.0 + lax.axis_index("col").astype(jnp.float32) / ndest)
         for at in range(len(pairs)):
             cut = slice(at * width, (at + 1) * width)
@@ -50,7 +51,7 @@
         out_ref[:, :, full - LANES :] = jnp.broadcast_to(power.reshape(1, 1, 1), (ndest, part, LANES))
 
 
-def tiles(lefts, rights, pairs, ndest, scaled=False):
+def tiles(lefts, rights, pairs, ndest, scaled=False, weigh=1):
     rows, depth = lefts[0].shape
     width = rows * len(pairs)
     return pl.pallas_call(
@@ -60,32 +61,38 @@
         out_shape=jax.ShapeDtypeStruct((ndest, rows // ndest, width + scaled * LANES), jnp.float32),
         compiler_params=ROOM,
         cost_estimate=pl.CostEstimate(
-            flops=2 * rows * width * depth,
+            flops=2 * rows * width * depth * weigh,
             bytes_accessed=2 * rows * depth * (len(lefts) + len(rights)) + 4 * rows * width,
             transcendentals=0,
         ),
     )(*lefts, *rights)
 
 
-def turn_kernel(first_ref, second_ref, own_ref, core_ref, half_ref, cross_ref, out_ref):
-    ndest, part, _ = out_ref.shape
+def power_of(most):
+    return jnp.floor(jnp.log2(LIMIT / jnp.maximum(most, 1e-33)))
+
+
+def summed(ref, first, count, powers):
+    ndest, part, _ = ref.shape
     width = ndest * part
-
-    def summed(ref):
-        full = ref.shape[2]
-        powers = [ref[source, :, full - LANES : full - LANES + 1] for source in range(ndest)]
-        weights = [jnp.exp2(-power) * (1.0 + source / ndest) for source, power in enumerate(powers)]
-
-        def total(at):
-            cut = slice(at * width, (at + 1) * width)
-            value = ref[0, :, cut] * weights[0]
-            for source in range(1, ndest):
-                value += ref[source, :, cut] * weights[source]
-            return value
-
-        return [total(at) for at in range(full // width)]
-
-    first, second = summed(first_ref), summed(second_ref)
+    weights = [
+        jnp.exp2(-ref[source, :, powers : powers + 1]) * (1.0 + source / ndest) for source in range(ndest)
+    ]
+    sums = []
+    for at in range(count):
+        cut = slice(first + at * width, first + (at + 1) * width)
+        value = ref[0, :, cut] * weights[0]
+        for source in range(1, ndest):
+            value += ref[source, :, cut] * weights[source]
+        sums.append(value)
+    return sums
+
+
+def turn_kernel(first_ref, second_ref, last_ref, own_ref, core_ref, half_ref, cross_ref, out_ref):
+    ndest, part, ahead = last_ref.shape
+    width = ndest * part
+    first = summed(first_ref, 0, 6, 6 * width)
+    second = summed(second_ref, 0, 10, 10 * width)
     for ref, blocks in (
         (own_ref, first[:3] + second[:1]),
         (core_ref, first[3:] + second[1:2]),
@@ -94,39 +101,58 @@
     ):
         for at, block in enumerate(blocks):
             ref[:, at * width : (at + 1) * width] = block
+    out_ref[:, :, :ahead] = last_ref[...]
     groups = (
         (first[1], first[4], second[3], second[7]),
         (first[2], first[5], second[4], second[8]),
         (second[0], second[1], second[5], second[9]),
     )
+    groups = [jnp.concatenate(group, axis=0) for group in groups]
+    most = jnp.maximum(jnp.maximum(jnp.abs(groups[0]), jnp.abs(groups[1])), jnp.abs(groups[2]))
+    power = power_of(jnp.max(jnp.max(most, axis=0, keepdims=True), axis=1, keepdims=True))
     step = 4 * part
     for at, group in enumerate(groups):
-        turned = jnp.concatenate(group, axis=0).T
-        out_ref[:, :, at * step : (at + 1) * step] = turned.reshape(ndest, part, step)
-
-
-def turn(first, second):
-    ndest, part, _ = first.shape
+        turned = group.T * jnp.exp2(power)
+        over = turned * SPLIT
+        high = over - (over - turned)
+        for start, piece in ((ahead, high), (ahead + 3 * step, turned - high)):
+            out_ref[:, :, start + at * step : start + (at + 1) * step] = piece.reshape(ndest, part, step)
+    out_ref[:, :, ahead + 6 * step :] = jnp.broadcast_to(power.reshape(1, 1, 1), (ndest, part, LANES))
+
+
+def turn(first, second, last):
+    ndest, part, ahead = last.shape
     width = ndest * part
     bundle = jax.ShapeDtypeStruct((part, 4 * width), jnp.float32)
     return pl.pallas_call(
         turn_kernel,
-        in_specs=[VMEM] * 2,
+        in_specs=[VMEM] * 3,
         out_specs=[VMEM] * 5,
-        out_shape=[bundle] * 4 + [jax.ShapeDtypeStruct((ndest, part, 12 * part), jnp.float32)],
-        compiler_params=ROOM,
-    )(first, second)
+        out_shape=[bundle] * 4 + [jax.ShapeDtypeStruct((ndest, part, ahead + 24 * part + LANES), jnp.float32)],
+        compiler_params=ROOM,
+    )(first, second, last)
 
 
 def settle_kernel(in_ref, *outs):
-    nsource, part, _ = in_ref.shape
+    nsource, part, full = in_ref.shape
     width = nsource * part
-    place = 0
+    ahead = 4 * width + LANES
+    opposite = summed(in_ref, 0, 4, 4 * width)
+    step = 4 * part
+    blocks = []
+    pieces = []
+    for source in range(nsource):
+        weight = jnp.exp2(-in_ref[source, :, full - LANES : full - LANES + 1])
+        high = in_ref[source, :, ahead : ahead + 3 * step]
+        low = in_ref[source, :, ahead + 3 * step : ahead + 6 * step]
+        pieces.append((high + low) * weight)
+    for place in range(12):
+        cut = slice(place * part, (place + 1) * part)
+        blocks.append(jnp.concatenate([piece[:, cut] for piece in pieces], axis=1))
+    blocks += opposite
     for ref in outs:
         for at in range(ref.shape[1] // width):
-            pieces = [in_ref[source, :, place * part : (place + 1) * part] for source in range(nsource)]
-            ref[:, at * width : (at + 1) * width] = jnp.concatenate(pieces, axis=1)
-            place += 1
+            ref[:, at * width : (at + 1) * width] = blocks.pop(0)
 
 
 def settle(turned):
@@ -135,8 +161,8 @@
     return pl.pallas_call(
         settle_kernel,
         in_specs=[VMEM],
-        out_specs=[VMEM] * 5,
-        out_shape=[jax.ShapeDtypeStruct((part, count * width), jnp.float32) for count in (4, 2, 2, 2, 2)],
+        out_specs=[VMEM] * 7,
+        out_shape=[jax.ShapeDtypeStruct((part, count * width), jnp.float32) for count in (4, 2, 2, 2, 2, 2, 2)],
         compiler_params=ROOM,
     )(turned)
 
@@ -183,18 +209,16 @@
 
     near = [(row, column) for row in range(2) for column in range(3)]
     first = tiles([down1, core1], [down1, gradient, up1], near, ncol, scaled=True)
-    half1 = hold(half1, first)
+    first = exchange(first.astype(jnp.float16))
+    half1 = hold(half1, first, up2, down2)
     cross1 = shift(half1, dc=1)
-    first = exchange(first.astype(jnp.float16))
-    up3, down3 = shift(hold(up2, first), dz=-1), shift(hold(down2, first), dz=1)
+    up3, down3 = shift(up2, dz=-1), shift(down2, dz=1)
     middle = [(0, 0), (1, 0)] + [(row, column) for row in (2, 3) for column in (1, 2, 3, 4)]
     second = tiles([down1, core1, half1, cross1], [up2, up1, gradient, down1, down2], middle, ncol, scaled=True)
     second = exchange(second.astype(jnp.float16))
-    own, core, half, cross, turned = turn(first.astype(jnp.float32), second.astype(jnp.float32))
-
-    last = tiles([up3, down3], [down1, core1, half1, cross1], [(0, 0), (0, 1), (1, 2), (1, 3)], ncol)
-    last = exchange(jnp.concatenate([last, turned], axis=2))
-    opposite, turned = last[:, :, : 4 * rows].sum(0), last[:, :, 4 * rows :]
+    last = tiles([up3, down3], [down1, core1, half1, cross1], [(0, 0), (0, 1), (1, 2), (1, 3)], ncol, scaled=True, weigh=40)
+    own, core, half, cross, last = turn(first.astype(jnp.float32), second.astype(jnp.float32), last)
+    last = exchange(last.astype(jnp.float16))
 
     home = [
         shift(own, dz=-1),
@@ -203,15 +227,15 @@
         shift(cross, dz=1, dy=1, dc=1),
     ]
     home_labels = [(k, d if k < 2 else -d) for k in range(4) for d in range(4)]
-    still, above1, below1, above2, below2 = settle(turned)
+    still, above1, below1, above2, below2, above3, below3 = settle(last.astype(jnp.float32))
     away = [
         still,
         shift(above1, dz=1),
         shift(below1, dz=-1),
         shift(above2, dz=2),
         shift(below2, dz=-2),
-        shift(opposite[:, : 2 * rows], dz=3),
-        shift(opposite[:, 2 * rows :], dz=-3),
+        shift(above3, dz=3),
+        shift(below3, dz=-3),
     ]
     away_labels = [(0, -1), (1, -1), (2, 1), (3, 1), (0, -2), (1, -2), (2, 2), (3, 2), (0, -3), (1, -3), (2, 3), (3, 3)]
     away_labels += [(k, 4) for k in range(4)]

time: 164 us -> 150 us (0.915)
  other arithmetic: 13.6 us -> 7.78 us
  starting transfers between devices: 46.9 us -> 42 us
  waiting for transfers between devices: 80.2 us -> 75.5 us
  local copies, waits for them, and re-layouts: 6.88 us -> 9.59 us
    ppermute x19, waiting for transfers between devices: 65.3 us -> 48.7 us  [shift(): return lax.ppermute(value, 'row', pairs)]
    all_to_all x3, waiting for transfers between devices: 14.9 us -> 26.9 us  [exchange(): return lax.all_to_all(parts, 'col', 0, 0, tiled=True)]
    add x4 -> x2, other arithmetic: 4.71 us -> 1.34 us  [hold(): value = value + (corner * 0).astype(value.dtype)]
    ppermute x19, starting transfers between devices: 31.7 us -> 28.8 us  [shift(): return lax.ppermute(value, 'row', pairs)]
    unnamed x16 -> x28, local copies, waits for them, and re-layouts: 2.9 us -> 5.41 us
    all_to_all x3, starting transfers between devices: 15.1 us -> 13.2 us  [exchange(): return lax.all_to_all(parts, 'col', 0, 0, tiled=True)]
    slice x3 -> x4, local copies, waits for them, and re-layouts: 2.95 us -> 4.18 us  [hold(): corner = other[(slice(0, 1),) * other.ndim].reshape(1, 1)]
  transfers between devices with their start and end apart: 22 -> 22, of which waited for: 8 -> 11; matrix products, arithmetic and copies ran while one was open for 9% -> 5% of each run, Pallas kernels for 7% -> 6%
where the time goes in v3:
time: 150 us; the launch traced here: 149 us
  waiting for transfers between devices  75.5 us (50%)
  starting transfers between devices  42 us (28%)
  Pallas kernels  11.7 us (8%)
  local copies, waits for them, and re-layouts  9.59 us (6%)
  other arithmetic  7.78 us (5%)
  between operations  2.84 us (2%)
    ppermute x19, waiting for transfers between devices, shift(): return lax.ppermute(value, 'row', pairs)  48.7 us
    ppermute x19, starting transfers between devices, shift(): return lax.ppermute(value, 'row', pairs)  28.8 us
    all_to_all x3, waiting for transfers between devices, exchange(): return lax.all_to_all(parts, 'col', 0, 0, tiled=True)  26.9 us
    all_to_all x3, starting transfers between devices, exchange(): return lax.all_to_all(parts, 'col', 0, 0, tiled=True)  13.2 us
    pallas_call x3, Pallas kernels, tiles(): pl.pallas_call(lambda *refs: tiles_kernel(len(lefts), len(rights), pairs,...  8.9 us
    unnamed x28, local copies, waits for them, and re-layouts  5.41 us
    slice x4, local copies, waits for them, and re-layouts, hold(): corner = other[(slice(0, 1),) * other.ndim].reshape(1, 1)  4.18 us
  transfers between devices with their start and end apart: 22, of which 11 were waited for; matrix products, arithmetic and copies ran while one was open for 5% of the time, Pallas kernels for 6%

profile of v3, /device:TPU:32, one launch (start us, length us, event | category | flops | bytes accessed | tf_op | source)
XLA Modules:
  0.0 149.4 jit_solution(546678210205384745)
XLA Ops:
  0.0 1.8 %collective-permute-start.1 = (bf16[256,1792]{1,0:T(8,128)(2,1)}, bf16[256,1792]{1,0:T(8,128)(2,1)S(1)}, u32[]{:S(2)}, u32[]{:S(2)}) collective-permute-start(bf16[256,1792]{1,0:T(8,128)(2,1)} %refs_6_.1), channel_id=1, source_target_pairs={{0,224},{8,232},{16,240},{24,248},{32,0},{40,8},{48,16},{56,24},{6... | collective-permute-start | bytes 2752520 | tf_op jit(solution)/shard_map/ppermute | solution.py:23
  2.0 20.5 %collective-permute-done.1.refs_4_.refs_5_ = bf16[256,1792]{1,0:T(8,128)(2,1)S(1)} collective-permute-done((bf16[256,1792]{1,0:T(8,128)(2,1)}, bf16[256,1792]{1,0:T(8,128)(2,1)S(1)}, u32[]{:S(2)}, u32[]{:S(2)}) %collective-permute-start.1) | collective-permute-done | bytes 917536 | tf_op jit(solution)/shard_map/ppermute | solution.py:23
  23.8 2.5 %collective-permute-done.refs_0_.refs_2_.refs_7_ = bf16[256,1792]{1,0:T(8,128)(2,1)S(1)} collective-permute-done((bf16[256,1792]{1,0:T(8,128)(2,1)}, bf16[256,1792]{1,0:T(8,128)(2,1)S(1)}, u32[]{:S(2)}, u32[]{:S(2)}) %collective-permute-start) | collective-permute-done | bytes 917536 | tf_op jit(solution)/shard_map/ppermute | solution.py:23
  26.4 3.0 %collective-permute-start.4 = (bf16[256,1792]{1,0:T(8,128)(2,1)S(1)}, bf16[256,1792]{1,0:T(8,128)(2,1)}, u32[]{:S(2)}, u32[]{:S(2)}) collective-permute-start(bf16[256,1792]{1,0:T(8,128)(2,1)S(1)} %collective-permute-done.1.refs_4_.refs_5_), channel_id=1, source_target_pairs={{0,224},{8,232},{16,240},{24,248},{32,0},{40,8},{48,16},{56,24},{6... | collective-permute-start | bytes 2752520 | tf_op jit(solution)/shard_map/ppermute | solution.py:23
  29.4 3.2 %collective-permute-start.3 = (bf16[256,1792]{1,0:T(8,128)(2,1)S(1)}, bf16[256,1792]{1,0:T(8,128)(2,1)}, u32[]{:S(2)}, u32[]{:S(2)}) collective-permute-start(bf16[256,1792]{1,0:T(8,128)(2,1)S(1)} %collective-permute-done.1.refs_4_.refs_5_), channel_id=1, source_target_pairs={{0,16},{8,24},{16,0},{24,8},{32,48},{40,56},{48,32},{56,40},{64,80... | collective-permute-start | bytes 2752520 | tf_op jit(solution)/shard_map/ppermute | solution.py:23
  32.6 1.8 %shard_map.37 = f32[8,32,1664]{2,1,0:T(8,128)S(1)} custom-call(bf16[256,1792]{1,0:T(8,128)(2,1)S(1)} %collective-permute-done.refs_0_.refs_2_.refs_7_, bf16[256,1792]{1,0:T(8,128)(2,1)S(1)} %collective-permute-done.2.refs_1_.refs_3_, bf16[256,1792]{1,0:T(8,128)(2,1)S(1)} %collective-permute-done.refs_0_.refs_2_.refs_7_, bf16[256,1792]{1,0:T(8,128)(2,1)S(1)} %copy-done, ...), custom_call_target="tpu_custom_call" | custom-call | flops 1409286144 | bytes 6160384 | tf_op jit(solution)/shard_map/pallas_call | solution.py:57
  36.5 4.4 %all-to-all-start = ((f16[8,32,1664]{2,1,0:T(8,128)(2,1)}), f16[8,32,1664]{2,1,0:T(8,128)(2,1)}, u32[]{:S(2)}, u32[]{:S(2)}) async-start(f16[8,32,1664]{2,1,0:T(8,128)(2,1)} %convert_element_type.22), calls=%async_computation | async-start | bytes 1703936 | tf_op jit(solution)/shard_map/all_to_all | solution.py:203
  40.9 8.8 %collective-permute-done.4.refs_4_ = bf16[256,1792]{1,0:T(8,128)(2,1)} collective-permute-done((bf16[256,1792]{1,0:T(8,128)(2,1)S(1)}, bf16[256,1792]{1,0:T(8,128)(2,1)}, u32[]{:S(2)}, u32[]{:S(2)}) %collective-permute-start.4) | collective-permute-done | bytes 917536 | tf_op jit(solution)/shard_map/ppermute | solution.py:23
  53.8 9.1 %all-to-all-done = f16[8,32,1664]{2,1,0:T(8,128)(2,1)} async-done(((f16[8,32,1664]{2,1,0:T(8,128)(2,1)}), f16[8,32,1664]{2,1,0:T(8,128)(2,1)}, u32[]{:S(2)}, u32[]{:S(2)}) %all-to-all-start) | async-done | bytes 852000 | tf_op jit(solution)/shard_map/all_to_all | solution.py:203
  69.7 4.3 %shard_map.38 = f32[8,32,2688]{2,1,0:T(8,128)S(1)} custom-call(bf16[256,1792]{1,0:T(8,128)(2,1)S(1)} %collective-permute-done.refs_0_.refs_2_.refs_7_, bf16[256,1792]{1,0:T(8,128)(2,1)S(1)} %copy-done.4, bf16[256,1792]{1,0:T(8,128)(2,1)S(1)} %add_add_fusion.refs_2_.refs_4_, bf16[256,1792]{1,0:T(8,128)(2,1)S(1)} %collective-permute-done.6.refs_3_.refs_5_, ...), custom_call_target="tpu_custom_call" | custom-call | flops 2348810240 | bytes 10878976 | tf_op jit(solution)/shard_map/pallas_call | solution.py:57
  76.2 5.2 %all-to-all-start.1 = ((f16[8,32,2688]{2,1,0:T(8,128)(2,1)}), f16[8,32,2688]{2,1,0:T(8,128)(2,1)}, u32[]{:S(2)}, u32[]{:S(2)}) async-start(f16[8,32,2688]{2,1,0:T(8,128)(2,1)} %convert_element_type.25), calls=%async_computation.1 | async-start | bytes 2752512 | tf_op jit(solution)/shard_map/all_to_all | solution.py:203
  81.4 7.9 %collective-permute-done.7.refs_0_ = bf16[256,1792]{1,0:T(8,128)(2,1)} collective-permute-done((bf16[256,1792]{1,0:T(8,128)(2,1)}, bf16[256,1792]{1,0:T(8,128)(2,1)}, u32[]{:S(2)}, u32[]{:S(2)}) %collective-permute-start.7) | collective-permute-done | bytes 917536 | tf_op jit(solution)/shard_map/ppermute | solution.py:23
  89.3 2.4 %collective-permute-done.8.refs_1_ = bf16[256,1792]{1,0:T(8,128)(2,1)} collective-permute-done((bf16[256,1792]{1,0:T(8,128)(2,1)}, bf16[256,1792]{1,0:T(8,128)(2,1)}, u32[]{:S(2)}, u32[]{:S(2)}) %collective-permute-start.8) | collective-permute-done | bytes 917536 | tf_op jit(solution)/shard_map/ppermute | solution.py:23
  94.1 2.8 %shard_map.39.last_ref = f32[8,32,1152]{2,1,0:T(8,128)S(1)} custom-call(bf16[256,1792]{1,0:T(8,128)(2,1)} %collective-permute-done.7.refs_0_, bf16[256,1792]{1,0:T(8,128)(2,1)} %collective-permute-done.8.refs_1_, bf16[256,1792]{1,0:T(8,128)(2,1)S(1)} %collective-permute-done.refs_0_.refs_2_.refs_7_, bf16[256,1792]{1,0:T(8,128)(2,1)S(1)} %copy-done.5, ...), custom_call_target="tpu_custom_call" | custom-call | flops 37580963840 | bytes 6553600 | tf_op jit(solution)/shard_map/pallas_call | solution.py:57
  97.9 4.6 %all-to-all-done.1 = f16[8,32,2688]{2,1,0:T(8,128)(2,1)} async-done(((f16[8,32,2688]{2,1,0:T(8,128)(2,1)}), f16[8,32,2688]{2,1,0:T(8,128)(2,1)}, u32[]{:S(2)}, u32[]{:S(2)}) %all-to-all-start.1) | async-done | bytes 1376288 | tf_op jit(solution)/shard_map/all_to_all | solution.py:203
  106.0 3.6 %all-to-all-start.2 = ((f16[8,32,2048]{2,1,0:T(8,128)(2,1)}), f16[8,32,2048]{2,1,0:T(8,128)(2,1)S(1)}, u32[]{:S(2)}, u32[]{:S(2)}) async-start(f16[8,32,2048]{2,1,0:T(8,128)(2,1)} %convert_element_type.27), calls=%async_computation.2 | async-start | bytes 2097152 | tf_op jit(solution)/shard_map/all_to_all | solution.py:203
  111.5 3.0 %collective-permute-start.12 = (f32[32,1024]{1,0:T(8,128)S(1)}, f32[32,1024]{1,0:T(8,128)S(1)}, u32[]{:S(2)}, u32[]{:S(2)}) collective-permute-start(f32[32,1024]{1,0:T(8,128)S(1)} %get-tuple-element.20), channel_id=1, source_target_pairs={{0,56},{8,48},{16,40},{24,32},{32,88},{40,80},{48,72},{56,64},{64,... | collective-permute-start | bytes 393224 | tf_op jit(solution)/shard_map/ppermute | solution.py:23
  115.6 13.1 %all-to-all-done.2 = f16[8,32,2048]{2,1,0:T(8,128)(2,1)S(1)} async-done(((f16[8,32,2048]{2,1,0:T(8,128)(2,1)}), f16[8,32,2048]{2,1,0:T(8,128)(2,1)S(1)}, u32[]{:S(2)}, u32[]{:S(2)}) %all-to-all-start.2) | async-done | bytes 1048608 | tf_op jit(solution)/shard_map/all_to_all | solution.py:203
  130.5 2.1 %collective-permute-start.14 = (f32[32,512]{1,0:T(8,128)S(1)}, f32[32,512]{1,0:T(8,128)S(1)}, u32[]{:S(2)}, u32[]{:S(2)}) collective-permute-start(f32[32,512]{1,0:T(8,128)S(1)} %get-tuple-element.24), channel_id=1, source_target_pairs={{0,224},{8,232},{16,240},{24,248},{32,0},{40,8},{48,16},{56,24},{6... | collective-permute-start | bytes 196616 | tf_op jit(solution)/shard_map/ppermute | solution.py:23
  132.5 2.0 %collective-permute-start.15 = (f32[32,512]{1,0:T(8,128)S(1)}, f32[32,512]{1,0:T(8,128)S(1)}, u32[]{:S(2)}, u32[]{:S(2)}) collective-permute-start(f32[32,512]{1,0:T(8,128)S(1)} %get-tuple-element.25), channel_id=1, source_target_pairs={{0,64},{8,72},{16,80},{24,88},{32,96},{40,104},{48,112},{56,120},{... | collective-permute-start | bytes 196616 | tf_op jit(solution)/shard_map/ppermute | solution.py:23
  134.5 2.1 %collective-permute-start.16 = (f32[32,512]{1,0:T(8,128)S(1)}, f32[32,512]{1,0:T(8,128)S(1)}, u32[]{:S(2)}, u32[]{:S(2)}) collective-permute-start(f32[32,512]{1,0:T(8,128)S(1)} %get-tuple-element.26), channel_id=1, source_target_pairs={{0,192},{8,200},{16,208},{24,216},{32,224},{40,232},{48,240},{56,2... | collective-permute-start | bytes 196616 | tf_op jit(solution)/shard_map/ppermute | solution.py:23
  136.7 3.3 %collective-permute-start.17 = (f32[32,512]{1,0:T(8,128)S(1)}, f32[32,512]{1,0:T(8,128)S(1)}, u32[]{:S(2)}, u32[]{:S(2)}) collective-permute-start(f32[32,512]{1,0:T(8,128)S(1)} %get-tuple-element.27), channel_id=1, source_target_pairs={{0,96},{8,104},{16,112},{24,120},{32,128},{40,136},{48,144},{56,15... | collective-permute-start | bytes 196616 | tf_op jit(solution)/shard_map/ppermute | solution.py:23
  141.8 2.2 %collective-permute-done.17.refs_9_ = f32[32,512]{1,0:T(8,128)S(1)} collective-permute-done((f32[32,512]{1,0:T(8,128)S(1)}, f32[32,512]{1,0:T(8,128)S(1)}, u32[]{:S(2)}, u32[]{:S(2)}) %collective-permute-start.17) | collective-permute-done | bytes 65568 | tf_op jit(solution)/shard_map/ppermute | solution.py:23
  143.9 3.9 %collective-permute-done.18.refs_10_ = f32[32,512]{1,0:T(8,128)S(1)} collective-permute-done((f32[32,512]{1,0:T(8,128)S(1)}, f32[32,512]{1,0:T(8,128)S(1)}, u32[]{:S(2)}, u32[]{:S(2)}) %collective-permute-start.18) | collective-permute-done | bytes 65568 | tf_op jit(solution)/shard_map/ppermute | solution.py:23
  (67 shorter events, 28.8 us)
Async XLA Ops:
  0.0 32.6 %copy-start = (bf16[256,1792]{1,0:T(8,128)(2,1)S(1)}, bf16[256,1792]{1,0:T(8,128)(2,1)}, u32[]{:S(2)}) copy-start(bf16[256,1792]{1,0:T(8,128)(2,1)} %refs_6_.1) | copy-start | bytes 2752516
  0.0 22.5 %collective-permute-start.1 = (bf16[256,1792]{1,0:T(8,128)(2,1)}, bf16[256,1792]{1,0:T(8,128)(2,1)S(1)}, u32[]{:S(2)}, u32[]{:S(2)}) collective-permute-start(bf16[256,1792]{1,0:T(8,128)(2,1)} %refs_6_.1), channel_id=1, source_target_pairs={{0,224},{8,232},{16,240},{24,248},{32,0},{40,8},{48,16},{56,24},{6... | collective-permute-start | bytes 2752520 | tf_op jit(solution)/shard_map/ppermute | solution.py:23
  1.8 24.4 %collective-permute-start = (bf16[256,1792]{1,0:T(8,128)(2,1)}, bf16[256,1792]{1,0:T(8,128)(2,1)S(1)}, u32[]{:S(2)}, u32[]{:S(2)}) collective-permute-start(bf16[256,1792]{1,0:T(8,128)(2,1)} %refs_6_.1), channel_id=1, source_target_pairs={{0,32},{8,40},{16,48},{24,56},{32,64},{40,72},{48,80},{56,88},{64,... | collective-permute-start | bytes 2752520 | tf_op jit(solution)/shard_map/ppermute | solution.py:23
  26.3 6.3 %collective-permute-start.2 = (bf16[256,1792]{1,0:T(8,128)(2,1)S(1)}, bf16[256,1792]{1,0:T(8,128)(2,1)S(1)}, u32[]{:S(2)}, u32[]{:S(2)}) collective-permute-start(bf16[256,1792]{1,0:T(8,128)(2,1)S(1)} %broadcast_add_fusion), channel_id=1, source_target_pairs={{0,8},{8,0},{16,24},{24,16},{32,40},{40,32},{48,56},{56,48},{64,72... | collective-permute-start | bytes 2752520 | tf_op jit(solution)/shard_map/ppermute | solution.py:23
  26.4 23.2 %collective-permute-start.4 = (bf16[256,1792]{1,0:T(8,128)(2,1)S(1)}, bf16[256,1792]{1,0:T(8,128)(2,1)}, u32[]{:S(2)}, u32[]{:S(2)}) collective-permute-start(bf16[256,1792]{1,0:T(8,128)(2,1)S(1)} %collective-permute-done.1.refs_4_.refs_5_), channel_id=1, source_target_pairs={{0,224},{8,232},{16,240},{24,248},{32,0},{40,8},{48,16},{56,24},{6... | collective-permute-start | bytes 2752520 | tf_op jit(solution)/shard_map/ppermute | solution.py:23
  29.4 22.5 %collective-permute-start.5 = (bf16[256,1792]{1,0:T(8,128)(2,1)S(1)}, bf16[256,1792]{1,0:T(8,128)(2,1)}, u32[]{:S(2)}, u32[]{:S(2)}) collective-permute-start(bf16[256,1792]{1,0:T(8,128)(2,1)S(1)} %collective-permute-done.refs_0_.refs_2_.refs_7_), channel_id=1, source_target_pairs={{0,32},{8,40},{16,48},{24,56},{32,64},{40,72},{48,80},{56,88},{64,... | collective-permute-start | bytes 2752520 | tf_op jit(solution)/shard_map/ppermute | solution.py:23
  29.4 35.4 %collective-permute-start.3 = (bf16[256,1792]{1,0:T(8,128)(2,1)S(1)}, bf16[256,1792]{1,0:T(8,128)(2,1)}, u32[]{:S(2)}, u32[]{:S(2)}) collective-permute-start(bf16[256,1792]{1,0:T(8,128)(2,1)S(1)} %collective-permute-done.1.refs_4_.refs_5_), channel_id=1, source_target_pairs={{0,16},{8,24},{16,0},{24,8},{32,48},{40,56},{48,32},{56,40},{64,80... | collective-permute-start | bytes 2752520 | tf_op jit(solution)/shard_map/ppermute | solution.py:23
  36.5 26.5 %all-to-all-start = ((f16[8,32,1664]{2,1,0:T(8,128)(2,1)}), f16[8,32,1664]{2,1,0:T(8,128)(2,1)}, u32[]{:S(2)}, u32[]{:S(2)}) async-start(f16[8,32,1664]{2,1,0:T(8,128)(2,1)} %convert_element_type.22), calls=%async_computation | async-start | bytes 1703936 | tf_op jit(solution)/shard_map/all_to_all | solution.py:203
  66.1 3.5 %collective-permute-start.6 = (bf16[256,1792]{1,0:T(8,128)(2,1)S(1)}, bf16[256,1792]{1,0:T(8,128)(2,1)S(1)}, u32[]{:S(2)}, u32[]{:S(2)}) collective-permute-start(bf16[256,1792]{1,0:T(8,128)(2,1)S(1)} %add_add_fusion.refs_2_.refs_4_), channel_id=1, source_target_pairs={{0,8},{8,0},{16,24},{24,16},{32,40},{40,32},{48,56},{56,48},{64,72... | collective-permute-start | bytes 2752520 | tf_op jit(solution)/shard_map/ppermute | solution.py:23
  66.2 23.1 %collective-permute-start.7 = (bf16[256,1792]{1,0:T(8,128)(2,1)}, bf16[256,1792]{1,0:T(8,128)(2,1)}, u32[]{:S(2)}, u32[]{:S(2)}) collective-permute-start(bf16[256,1792]{1,0:T(8,128)(2,1)} %collective-permute-done.4.refs_4_), channel_id=1, source_target_pairs={{0,224},{8,232},{16,240},{24,248},{32,0},{40,8},{48,16},{56,24},{6... | collective-permute-start | bytes 2752520 | tf_op jit(solution)/shard_map/ppermute | solution.py:23
  68.1 23.7 %collective-permute-start.8 = (bf16[256,1792]{1,0:T(8,128)(2,1)}, bf16[256,1792]{1,0:T(8,128)(2,1)}, u32[]{:S(2)}, u32[]{:S(2)}) collective-permute-start(bf16[256,1792]{1,0:T(8,128)(2,1)} %collective-permute-done.5.refs_8_), channel_id=1, source_target_pairs={{0,32},{8,40},{16,48},{24,56},{32,64},{40,72},{48,80},{56,88},{64,... | collective-permute-start | bytes 2752520 | tf_op jit(solution)/shard_map/ppermute | solution.py:23
  76.2 15.5 %copy-start.5 = (bf16[256,1792]{1,0:T(8,128)(2,1)S(1)}, bf16[256,1792]{1,0:T(8,128)(2,1)}, u32[]{:S(2)}) copy-start(bf16[256,1792]{1,0:T(8,128)(2,1)} %copy-done.3) | copy-start | bytes 2752516
  76.2 26.3 %all-to-all-start.1 = ((f16[8,32,2688]{2,1,0:T(8,128)(2,1)}), f16[8,32,2688]{2,1,0:T(8,128)(2,1)}, u32[]{:S(2)}, u32[]{:S(2)}) async-start(f16[8,32,2688]{2,1,0:T(8,128)(2,1)} %convert_element_type.25), calls=%async_computation.1 | async-start | bytes 2752512 | tf_op jit(solution)/shard_map/all_to_all | solution.py:203
  106.0 22.7 %all-to-all-start.2 = ((f16[8,32,2048]{2,1,0:T(8,128)(2,1)}), f16[8,32,2048]{2,1,0:T(8,128)(2,1)S(1)}, u32[]{:S(2)}, u32[]{:S(2)}) async-start(f16[8,32,2048]{2,1,0:T(8,128)(2,1)} %convert_element_type.27), calls=%async_computation.2 | async-start | bytes 2097152 | tf_op jit(solution)/shard_map/all_to_all | solution.py:203
  109.6 20.9 %collective-permute-start.10 = (f32[32,1024]{1,0:T(8,128)S(1)}, f32[32,1024]{1,0:T(8,128)S(1)}, u32[]{:S(2)}, u32[]{:S(2)}) collective-permute-start(f32[32,1024]{1,0:T(8,128)S(1)} %get-tuple-element.18), channel_id=1, source_target_pairs={{0,232},{8,224},{16,248},{24,240},{32,8},{40,0},{48,24},{56,16},{6... | collective-permute-start | bytes 393224 | tf_op jit(solution)/shard_map/ppermute | solution.py:23
  111.2 21.3 %collective-permute-start.11 = (f32[32,1024]{1,0:T(8,128)S(1)}, f32[32,1024]{1,0:T(8,128)S(1)}, u32[]{:S(2)}, u32[]{:S(2)}) collective-permute-start(f32[32,1024]{1,0:T(8,128)S(1)} %get-tuple-element.19), channel_id=1, source_target_pairs={{0,48},{8,56},{16,32},{24,40},{32,80},{40,88},{48,64},{56,72},{64,... | collective-permute-start | bytes 393224 | tf_op jit(solution)/shard_map/ppermute | solution.py:23
  111.5 23.0 %collective-permute-start.12 = (f32[32,1024]{1,0:T(8,128)S(1)}, f32[32,1024]{1,0:T(8,128)S(1)}, u32[]{:S(2)}, u32[]{:S(2)}) collective-permute-start(f32[32,1024]{1,0:T(8,128)S(1)} %get-tuple-element.20), channel_id=1, source_target_pairs={{0,56},{8,48},{16,40},{24,32},{32,88},{40,80},{48,72},{56,64},{64,... | collective-permute-start | bytes 393224 | tf_op jit(solution)/shard_map/ppermute | solution.py:23
  114.5 22.2 %collective-permute-start.9 = (f32[32,1024]{1,0:T(8,128)S(1)}, f32[32,1024]{1,0:T(8,128)S(1)}, u32[]{:S(2)}, u32[]{:S(2)}) collective-permute-start(f32[32,1024]{1,0:T(8,128)S(1)} %get-tuple-element.17), channel_id=1, source_target_pairs={{0,224},{8,232},{16,240},{24,248},{32,0},{40,8},{48,16},{56,24},{6... | collective-permute-start | bytes 393224 | tf_op jit(solution)/shard_map/ppermute | solution.py:23
  129.4 10.6 %collective-permute-start.13 = (f32[32,512]{1,0:T(8,128)S(1)}, f32[32,512]{1,0:T(8,128)S(1)}, u32[]{:S(2)}, u32[]{:S(2)}) collective-permute-start(f32[32,512]{1,0:T(8,128)S(1)} %get-tuple-element.23), channel_id=1, source_target_pairs={{0,32},{8,40},{16,48},{24,56},{32,64},{40,72},{48,80},{56,88},{64,... | collective-permute-start | bytes 196616 | tf_op jit(solution)/shard_map/ppermute | solution.py:23
  130.5 11.3 %collective-permute-start.14 = (f32[32,512]{1,0:T(8,128)S(1)}, f32[32,512]{1,0:T(8,128)S(1)}, u32[]{:S(2)}, u32[]{:S(2)}) collective-permute-start(f32[32,512]{1,0:T(8,128)S(1)} %get-tuple-element.24), channel_id=1, source_target_pairs={{0,224},{8,232},{16,240},{24,248},{32,0},{40,8},{48,16},{56,24},{6... | collective-permute-start | bytes 196616 | tf_op jit(solution)/shard_map/ppermute | solution.py:23
  132.5 9.2 %collective-permute-start.15 = (f32[32,512]{1,0:T(8,128)S(1)}, f32[32,512]{1,0:T(8,128)S(1)}, u32[]{:S(2)}, u32[]{:S(2)}) collective-permute-start(f32[32,512]{1,0:T(8,128)S(1)} %get-tuple-element.25), channel_id=1, source_target_pairs={{0,64},{8,72},{16,80},{24,88},{32,96},{40,104},{48,112},{56,120},{... | collective-permute-start | bytes 196616 | tf_op jit(solution)/shard_map/ppermute | solution.py:23
  134.5 7.2 %collective-permute-start.16 = (f32[32,512]{1,0:T(8,128)S(1)}, f32[32,512]{1,0:T(8,128)S(1)}, u32[]{:S(2)}, u32[]{:S(2)}) collective-permute-start(f32[32,512]{1,0:T(8,128)S(1)} %get-tuple-element.26), channel_id=1, source_target_pairs={{0,192},{8,200},{16,208},{24,216},{32,224},{40,232},{48,240},{56,2... | collective-permute-start | bytes 196616 | tf_op jit(solution)/shard_map/ppermute | solution.py:23
  136.7 7.3 %collective-permute-start.17 = (f32[32,512]{1,0:T(8,128)S(1)}, f32[32,512]{1,0:T(8,128)S(1)}, u32[]{:S(2)}, u32[]{:S(2)}) collective-permute-start(f32[32,512]{1,0:T(8,128)S(1)} %get-tuple-element.27), channel_id=1, source_target_pairs={{0,96},{8,104},{16,112},{24,120},{32,128},{40,136},{48,144},{56,15... | collective-permute-start | bytes 196616 | tf_op jit(solution)/shard_map/ppermute | solution.py:23
  140.0 7.8 %collective-permute-start.18 = (f32[32,512]{1,0:T(8,128)S(1)}, f32[32,512]{1,0:T(8,128)S(1)}, u32[]{:S(2)}, u32[]{:S(2)}) collective-permute-start(f32[32,512]{1,0:T(8,128)S(1)} %get-tuple-element.28), channel_id=1, source_target_pairs={{0,160},{8,168},{16,176},{24,184},{32,192},{40,200},{48,208},{56,2... | collective-permute-start | bytes 196616 | tf_op jit(solution)/shard_map/ppermute | solution.py:23
  (12 other events, 59.5 us)

commit v4 on v3

--- a/solution.py
+++ b/solution.py
@@ -204,13 +204,13 @@
 
     up1, down1 = shift(gradient, dz=-1), shift(gradient, dz=1)
     half1 = shift(up1, dy=1)
-    core1 = shift(hold(down1, up1), dc=1)
+    core1 = shift(down1, dc=1)
     up2, down2 = shift(up1, dz=-1), shift(down1, dz=1)
 
     near = [(row, column) for row in range(2) for column in range(3)]
     first = tiles([down1, core1], [down1, gradient, up1], near, ncol, scaled=True)
     first = exchange(first.astype(jnp.float16))
-    half1 = hold(half1, first, up2, down2)
+    half1 = hold(half1, first)
     cross1 = shift(half1, dc=1)
     up3, down3 = shift(up2, dz=-1), shift(down2, dz=1)
     middle = [(0, 0), (1, 0)] + [(row, column) for row in (2, 3) for column in (1, 2, 3, 4)]

time: 150 us -> 148 us (0.987)
  local copies, waits for them, and re-layouts: 9.59 us -> 6.75 us
  starting transfers between devices: 42 us -> 44.6 us
  between operations: 2.84 us -> 0.83 us
    all_to_all x3, waiting for transfers between devices: 26.9 us -> 36.2 us  [exchange(): return lax.all_to_all(parts, 'col', 0, 0, tiled=True)]
    ppermute x19, waiting for transfers between devices: 48.7 us -> 39.6 us  [shift(): return lax.ppermute(value, 'row', pairs)]
    slice x4 -> x1, local copies, waits for them, and re-layouts: 4.18 us -> 1.19 us  [hold(): corner = other[(slice(0, 1),) * other.ndim].reshape(1, 1)]
    ppermute x19, starting transfers between devices: 28.8 us -> 31.6 us  [shift(): return lax.ppermute(value, 'row', pairs)]
    unnamed x28 -> x24, local copies, waits for them, and re-layouts: 5.41 us -> 5.56 us
  transfers between devices with their start and end apart: 22 -> 22, of which waited for: 11 -> 9; matrix products, arithmetic and copies ran while one was open for 5% -> 4% of each run, Pallas kernels for 6% -> 6%
where the time goes in v4:
time: 148 us; the launch traced here: 147 us
  waiting for transfers between devices  75.8 us (51%)
  starting transfers between devices  44.6 us (30%)
  Pallas kernels  11.7 us (8%)
  other arithmetic  7.64 us (5%)
  local copies, waits for them, and re-layouts  6.75 us (5%)
    ppermute x19, waiting for transfers between devices, shift(): return lax.ppermute(value, 'row', pairs)  39.6 us
    all_to_all x3, waiting for transfers between devices, exchange(): return lax.all_to_all(parts, 'col', 0, 0, tiled=True)  36.2 us
    ppermute x19, starting transfers between devices, shift(): return lax.ppermute(value, 'row', pairs)  31.6 us
    all_to_all x3, starting transfers between devices, exchange(): return lax.all_to_all(parts, 'col', 0, 0, tiled=True)  13.1 us
    pallas_call x3, Pallas kernels, tiles(): pl.pallas_call(lambda *refs: tiles_kernel(len(lefts), len(rights), pairs,...  8.9 us
    unnamed x24, local copies, waits for them, and re-layouts  5.56 us
  transfers between devices with their start and end apart: 22, of which 9 were waited for; matrix products, arithmetic and copies ran while one was open for 4% of the time, Pallas kernels for 6%

profile of v4, /device:TPU:32, one launch (start us, length us, event | category | flops | bytes accessed | tf_op | source)
XLA Modules:
  0.0 147.3 jit_solution(7537539529186870575)
XLA Ops:
  0.0 1.9 %collective-permute-start = (bf16[256,1792]{1,0:T(8,128)(2,1)}, bf16[256,1792]{1,0:T(8,128)(2,1)S(1)}, u32[]{:S(2)}, u32[]{:S(2)}) collective-permute-start(bf16[256,1792]{1,0:T(8,128)(2,1)} %refs_6_.1), channel_id=1, source_target_pairs={{0,32},{8,40},{16,48},{24,56},{32,64},{40,72},{48,80},{56,88},{64,... | collective-permute-start | bytes 2752520 | tf_op jit(solution)/shard_map/ppermute | solution.py:23
  2.0 20.3 %collective-permute-done.refs_0_.refs_2_.refs_7_ = bf16[256,1792]{1,0:T(8,128)(2,1)S(1)} collective-permute-done((bf16[256,1792]{1,0:T(8,128)(2,1)}, bf16[256,1792]{1,0:T(8,128)(2,1)S(1)}, u32[]{:S(2)}, u32[]{:S(2)}) %collective-permute-start) | collective-permute-done | bytes 917536 | tf_op jit(solution)/shard_map/ppermute | solution.py:23
  22.3 1.8 %collective-permute-done.2.refs_4_.refs_5_ = bf16[256,1792]{1,0:T(8,128)(2,1)S(1)} collective-permute-done((bf16[256,1792]{1,0:T(8,128)(2,1)}, bf16[256,1792]{1,0:T(8,128)(2,1)S(1)}, u32[]{:S(2)}, u32[]{:S(2)}) %collective-permute-start.2) | collective-permute-done | bytes 917536 | tf_op jit(solution)/shard_map/ppermute | solution.py:23
  24.1 3.2 %collective-permute-start.3 = (bf16[256,1792]{1,0:T(8,128)(2,1)S(1)}, bf16[256,1792]{1,0:T(8,128)(2,1)}, u32[]{:S(2)}, u32[]{:S(2)}) collective-permute-start(bf16[256,1792]{1,0:T(8,128)(2,1)S(1)} %collective-permute-done.2.refs_4_.refs_5_), channel_id=1, source_target_pairs={{0,16},{8,24},{16,0},{24,8},{32,48},{40,56},{48,32},{56,40},{64,80... | collective-permute-start | bytes 2752520 | tf_op jit(solution)/shard_map/ppermute | solution.py:23
  28.5 1.8 %shard_map.37 = f32[8,32,1664]{2,1,0:T(8,128)S(1)} custom-call(bf16[256,1792]{1,0:T(8,128)(2,1)S(1)} %collective-permute-done.refs_0_.refs_2_.refs_7_, bf16[256,1792]{1,0:T(8,128)(2,1)S(1)} %collective-permute-done.1.refs_1_.refs_3_, bf16[256,1792]{1,0:T(8,128)(2,1)S(1)} %collective-permute-done.refs_0_.refs_2_.refs_7_, bf16[256,1792]{1,0:T(8,128)(2,1)S(1)} %copy-done, ...), custom_call_target="tpu_custom_call" | custom-call | flops 1409286144 | bytes 6160384 | tf_op jit(solution)/shard_map/pallas_call | solution.py:57
  31.4 4.4 %all-to-all-start = ((f16[8,32,1664]{2,1,0:T(8,128)(2,1)}), f16[8,32,1664]{2,1,0:T(8,128)(2,1)}, u32[]{:S(2)}, u32[]{:S(2)}) async-start(f16[8,32,1664]{2,1,0:T(8,128)(2,1)} %convert_element_type.22), calls=%async_computation | async-start | bytes 1703936 | tf_op jit(solution)/shard_map/all_to_all | solution.py:203
  35.8 3.1 %collective-permute-start.6 = (bf16[256,1792]{1,0:T(8,128)(2,1)S(1)}, bf16[256,1792]{1,0:T(8,128)(2,1)}, u32[]{:S(2)}, u32[]{:S(2)}) collective-permute-start(bf16[256,1792]{1,0:T(8,128)(2,1)S(1)} %collective-permute-done.refs_0_.refs_2_.refs_7_), channel_id=1, source_target_pairs={{0,32},{8,40},{16,48},{24,56},{32,64},{40,72},{48,80},{56,88},{64,... | collective-permute-start | bytes 2752520 | tf_op jit(solution)/shard_map/ppermute | solution.py:23
  38.9 17.4 %all-to-all-done = f16[8,32,1664]{2,1,0:T(8,128)(2,1)} async-done(((f16[8,32,1664]{2,1,0:T(8,128)(2,1)}), f16[8,32,1664]{2,1,0:T(8,128)(2,1)}, u32[]{:S(2)}, u32[]{:S(2)}) %all-to-all-start) | async-done | bytes 852000 | tf_op jit(solution)/shard_map/all_to_all | solution.py:203
  59.5 3.3 %collective-permute-start.8 = (bf16[256,1792]{1,0:T(8,128)(2,1)}, bf16[256,1792]{1,0:T(8,128)(2,1)}, u32[]{:S(2)}, u32[]{:S(2)}) collective-permute-start(bf16[256,1792]{1,0:T(8,128)(2,1)} %collective-permute-done.6.refs_8_), channel_id=1, source_target_pairs={{0,32},{8,40},{16,48},{24,56},{32,64},{40,72},{48,80},{56,88},{64,... | collective-permute-start | bytes 2752520 | tf_op jit(solution)/shard_map/ppermute | solution.py:23
  65.1 4.3 %shard_map.38 = f32[8,32,2688]{2,1,0:T(8,128)S(1)} custom-call(bf16[256,1792]{1,0:T(8,128)(2,1)S(1)} %collective-permute-done.refs_0_.refs_2_.refs_7_, bf16[256,1792]{1,0:T(8,128)(2,1)S(1)} %collective-permute-done.1.refs_1_.refs_3_, bf16[256,1792]{1,0:T(8,128)(2,1)S(1)} %broadcast_add_fusion.refs_2_.refs_4_, ...), custom_call_target="tpu_custom_call" | custom-call | flops 2348810240 | bytes 10878976 | tf_op jit(solution)/shard_map/pallas_call | solution.py:57
  71.5 5.1 %all-to-all-start.1 = ((f16[8,32,2688]{2,1,0:T(8,128)(2,1)}), f16[8,32,2688]{2,1,0:T(8,128)(2,1)}, u32[]{:S(2)}, u32[]{:S(2)}) async-start(f16[8,32,2688]{2,1,0:T(8,128)(2,1)} %convert_element_type.25), calls=%async_computation.1 | async-start | bytes 2752512 | tf_op jit(solution)/shard_map/all_to_all | solution.py:203
  76.6 8.3 %collective-permute-done.8.refs_1_ = bf16[256,1792]{1,0:T(8,128)(2,1)} collective-permute-done((bf16[256,1792]{1,0:T(8,128)(2,1)}, bf16[256,1792]{1,0:T(8,128)(2,1)}, u32[]{:S(2)}, u32[]{:S(2)}) %collective-permute-start.8) | collective-permute-done | bytes 917536 | tf_op jit(solution)/shard_map/ppermute | solution.py:23
  88.8 2.8 %shard_map.39.last_ref = f32[8,32,1152]{2,1,0:T(8,128)S(1)} custom-call(bf16[256,1792]{1,0:T(8,128)(2,1)} %collective-permute-done.7.refs_0_, bf16[256,1792]{1,0:T(8,128)(2,1)} %collective-permute-done.8.refs_1_, bf16[256,1792]{1,0:T(8,128)(2,1)S(1)} %collective-permute-done.refs_0_.refs_2_.refs_7_, ...), custom_call_target="tpu_custom_call" | custom-call | flops 37580963840 | bytes 6553600 | tf_op jit(solution)/shard_map/pallas_call | solution.py:57
  92.6 5.6 %all-to-all-done.1 = f16[8,32,2688]{2,1,0:T(8,128)(2,1)} async-done(((f16[8,32,2688]{2,1,0:T(8,128)(2,1)}), f16[8,32,2688]{2,1,0:T(8,128)(2,1)}, u32[]{:S(2)}, u32[]{:S(2)}) %all-to-all-start.1) | async-done | bytes 1376288 | tf_op jit(solution)/shard_map/all_to_all | solution.py:203
  98.2 1.6 %convert_element_type.26.second_ref = f32[8,32,2688]{2,1,0:T(8,128)S(1)} convert(f16[8,32,2688]{2,1,0:T(8,128)(2,1)} %all-to-all-done.1) | non-fusion elementwise | flops 688128 | bytes 4128768 | tf_op jit(solution)/shard_map/convert_element_type | solution.py:220
  101.7 3.6 %all-to-all-start.2 = ((f16[8,32,2048]{2,1,0:T(8,128)(2,1)}), f16[8,32,2048]{2,1,0:T(8,128)(2,1)S(1)}, u32[]{:S(2)}, u32[]{:S(2)}) async-start(f16[8,32,2048]{2,1,0:T(8,128)(2,1)} %convert_element_type.27), calls=%async_computation.2 | async-start | bytes 2097152 | tf_op jit(solution)/shard_map/all_to_all | solution.py:203
  107.9 3.0 %collective-permute-start.12 = (f32[32,1024]{1,0:T(8,128)S(1)}, f32[32,1024]{1,0:T(8,128)S(1)}, u32[]{:S(2)}, u32[]{:S(2)}) collective-permute-start(f32[32,1024]{1,0:T(8,128)S(1)} %get-tuple-element.20), channel_id=1, source_target_pairs={{0,56},{8,48},{16,40},{24,32},{32,88},{40,80},{48,72},{56,64},{64,... | collective-permute-start | bytes 393224 | tf_op jit(solution)/shard_map/ppermute | solution.py:23
  111.2 13.1 %all-to-all-done.2 = f16[8,32,2048]{2,1,0:T(8,128)(2,1)S(1)} async-done(((f16[8,32,2048]{2,1,0:T(8,128)(2,1)}), f16[8,32,2048]{2,1,0:T(8,128)(2,1)S(1)}, u32[]{:S(2)}, u32[]{:S(2)}) %all-to-all-start.2) | async-done | bytes 1048608 | tf_op jit(solution)/shard_map/all_to_all | solution.py:203
  125.0 1.8 %collective-permute-start.13 = (f32[32,512]{1,0:T(8,128)S(1)}, f32[32,512]{1,0:T(8,128)S(1)}, u32[]{:S(2)}, u32[]{:S(2)}) collective-permute-start(f32[32,512]{1,0:T(8,128)S(1)} %get-tuple-element.23), channel_id=1, source_target_pairs={{0,32},{8,40},{16,48},{24,56},{32,64},{40,72},{48,80},{56,88},{64,... | collective-permute-start | bytes 196616 | tf_op jit(solution)/shard_map/ppermute | solution.py:23
  127.9 3.4 %collective-permute-start.15 = (f32[32,512]{1,0:T(8,128)S(1)}, f32[32,512]{1,0:T(8,128)S(1)}, u32[]{:S(2)}, u32[]{:S(2)}) collective-permute-start(f32[32,512]{1,0:T(8,128)S(1)} %get-tuple-element.25), channel_id=1, source_target_pairs={{0,64},{8,72},{16,80},{24,88},{32,96},{40,104},{48,112},{56,120},{... | collective-permute-start | bytes 196616 | tf_op jit(solution)/shard_map/ppermute | solution.py:23
  132.1 5.9 %collective-permute-start.17 = (f32[32,512]{1,0:T(8,128)S(1)}, f32[32,512]{1,0:T(8,128)S(1)}, u32[]{:S(2)}, u32[]{:S(2)}) collective-permute-start(f32[32,512]{1,0:T(8,128)S(1)} %get-tuple-element.27), channel_id=1, source_target_pairs={{0,96},{8,104},{16,112},{24,120},{32,128},{40,136},{48,144},{56,15... | collective-permute-start | bytes 196616 | tf_op jit(solution)/shard_map/ppermute | solution.py:23
  138.1 1.9 %collective-permute-done.17.refs_9_ = f32[32,512]{1,0:T(8,128)S(1)} collective-permute-done((f32[32,512]{1,0:T(8,128)S(1)}, f32[32,512]{1,0:T(8,128)S(1)}, u32[]{:S(2)}, u32[]{:S(2)}) %collective-permute-start.17) | collective-permute-done | bytes 65568 | tf_op jit(solution)/shard_map/ppermute | solution.py:23
  140.0 5.7 %collective-permute-done.18.refs_10_ = f32[32,512]{1,0:T(8,128)S(1)} collective-permute-done((f32[32,512]{1,0:T(8,128)S(1)}, f32[32,512]{1,0:T(8,128)S(1)}, u32[]{:S(2)}, u32[]{:S(2)}) %collective-permute-start.18) | collective-permute-done | bytes 65568 | tf_op jit(solution)/shard_map/ppermute | solution.py:23
  145.7 1.6 %shard_map.42 = f32[32,8192]{1,0:T(8,128)} custom-call(s32[32]{0:T(128)S(1)} %fusion.2.to_ref, f32[32,1024]{1,0:T(8,128)S(1)} %collective-permute-done.9.refs_0_, f32[32,1024]{1,0:T(8,128)S(1)} %collective-permute-done.10.refs_1_, f32[32,1024]{1,0:T(8,128)S(1)} %collective-permute-done.11.refs_2_, f32[32,1024]{1,0:T(8,128)S(1)} %collective-permute-done.12.refs_3_, ...), custom_call_target="tpu_custom_call" | custom-call | tf_op jit(solution)/shard_map/pallas_call | solution.py:186
  (59 shorter events, 21.5 us)
Async XLA Ops:
  0.0 22.3 %collective-permute-start = (bf16[256,1792]{1,0:T(8,128)(2,1)}, bf16[256,1792]{1,0:T(8,128)(2,1)S(1)}, u32[]{:S(2)}, u32[]{:S(2)}) collective-permute-start(bf16[256,1792]{1,0:T(8,128)(2,1)} %refs_6_.1), channel_id=1, source_target_pairs={{0,32},{8,40},{16,48},{24,56},{32,64},{40,72},{48,80},{56,88},{64,... | collective-permute-start | bytes 2752520 | tf_op jit(solution)/shard_map/ppermute | solution.py:23
  1.9 22.2 %collective-permute-start.2 = (bf16[256,1792]{1,0:T(8,128)(2,1)}, bf16[256,1792]{1,0:T(8,128)(2,1)S(1)}, u32[]{:S(2)}, u32[]{:S(2)}) collective-permute-start(bf16[256,1792]{1,0:T(8,128)(2,1)} %refs_6_.1), channel_id=1, source_target_pairs={{0,224},{8,232},{16,240},{24,248},{32,0},{40,8},{48,16},{56,24},{6... | collective-permute-start | bytes 2752520 | tf_op jit(solution)/shard_map/ppermute | solution.py:23
  22.3 5.0 %collective-permute-start.1 = (bf16[256,1792]{1,0:T(8,128)(2,1)S(1)}, bf16[256,1792]{1,0:T(8,128)(2,1)S(1)}, u32[]{:S(2)}, u32[]{:S(2)}) collective-permute-start(bf16[256,1792]{1,0:T(8,128)(2,1)S(1)} %collective-permute-done.refs_0_.refs_2_.refs_7_), channel_id=1, source_target_pairs={{0,8},{8,0},{16,24},{24,16},{32,40},{40,32},{48,56},{56,48},{64,72... | collective-permute-start | bytes 2752520 | tf_op jit(solution)/shard_map/ppermute | solution.py:23
  24.1 14.8 %copy-start.2 = (bf16[256,1792]{1,0:T(8,128)(2,1)}, bf16[256,1792]{1,0:T(8,128)(2,1)S(1)}, u32[]{:S(2)}) copy-start(bf16[256,1792]{1,0:T(8,128)(2,1)S(1)} %collective-permute-done.2.refs_4_.refs_5_) | copy-start | bytes 2752516
  24.1 34.0 %collective-permute-start.3 = (bf16[256,1792]{1,0:T(8,128)(2,1)S(1)}, bf16[256,1792]{1,0:T(8,128)(2,1)}, u32[]{:S(2)}, u32[]{:S(2)}) collective-permute-start(bf16[256,1792]{1,0:T(8,128)(2,1)S(1)} %collective-permute-done.2.refs_4_.refs_5_), channel_id=1, source_target_pairs={{0,16},{8,24},{16,0},{24,8},{32,48},{40,56},{48,32},{56,40},{64,80... | collective-permute-start | bytes 2752520 | tf_op jit(solution)/shard_map/ppermute | solution.py:23
  31.4 25.0 %all-to-all-start = ((f16[8,32,1664]{2,1,0:T(8,128)(2,1)}), f16[8,32,1664]{2,1,0:T(8,128)(2,1)}, u32[]{:S(2)}, u32[]{:S(2)}) async-start(f16[8,32,1664]{2,1,0:T(8,128)(2,1)} %convert_element_type.22), calls=%async_computation | async-start | bytes 1703936 | tf_op jit(solution)/shard_map/all_to_all | solution.py:203
  35.8 23.7 %collective-permute-start.6 = (bf16[256,1792]{1,0:T(8,128)(2,1)S(1)}, bf16[256,1792]{1,0:T(8,128)(2,1)}, u32[]{:S(2)}, u32[]{:S(2)}) collective-permute-start(bf16[256,1792]{1,0:T(8,128)(2,1)S(1)} %collective-permute-done.refs_0_.refs_2_.refs_7_), channel_id=1, source_target_pairs={{0,32},{8,40},{16,48},{24,56},{32,64},{40,72},{48,80},{56,88},{64,... | collective-permute-start | bytes 2752520 | tf_op jit(solution)/shard_map/ppermute | solution.py:23
  38.9 23.9 %collective-permute-start.5 = (bf16[256,1792]{1,0:T(8,128)(2,1)S(1)}, bf16[256,1792]{1,0:T(8,128)(2,1)}, u32[]{:S(2)}, u32[]{:S(2)}) collective-permute-start(bf16[256,1792]{1,0:T(8,128)(2,1)S(1)} %collective-permute-done.2.refs_4_.refs_5_), channel_id=1, source_target_pairs={{0,224},{8,232},{16,240},{24,248},{32,0},{40,8},{48,16},{56,24},{6... | collective-permute-start | bytes 2752520 | tf_op jit(solution)/shard_map/ppermute | solution.py:23
  59.4 5.6 %collective-permute-start.4 = (bf16[256,1792]{1,0:T(8,128)(2,1)S(1)}, bf16[256,1792]{1,0:T(8,128)(2,1)S(1)}, u32[]{:S(2)}, u32[]{:S(2)}) collective-permute-start(bf16[256,1792]{1,0:T(8,128)(2,1)S(1)} %broadcast_add_fusion.refs_2_.refs_4_), channel_id=1, source_target_pairs={{0,8},{8,0},{16,24},{24,16},{32,40},{40,32},{48,56},{56,48},{64,72... | collective-permute-start | bytes 2752520 | tf_op jit(solution)/shard_map/ppermute | solution.py:23
  59.5 25.3 %collective-permute-start.8 = (bf16[256,1792]{1,0:T(8,128)(2,1)}, bf16[256,1792]{1,0:T(8,128)(2,1)}, u32[]{:S(2)}, u32[]{:S(2)}) collective-permute-start(bf16[256,1792]{1,0:T(8,128)(2,1)} %collective-permute-done.6.refs_8_), channel_id=1, source_target_pairs={{0,32},{8,40},{16,48},{24,56},{32,64},{40,72},{48,80},{56,88},{64,... | collective-permute-start | bytes 2752520 | tf_op jit(solution)/shard_map/ppermute | solution.py:23
  62.8 23.6 %collective-permute-start.7 = (bf16[256,1792]{1,0:T(8,128)(2,1)}, bf16[256,1792]{1,0:T(8,128)(2,1)}, u32[]{:S(2)}, u32[]{:S(2)}) collective-permute-start(bf16[256,1792]{1,0:T(8,128)(2,1)} %collective-permute-done.5.refs_4_), channel_id=1, source_target_pairs={{0,224},{8,232},{16,240},{24,248},{32,0},{40,8},{48,16},{56,24},{6... | collective-permute-start | bytes 2752520 | tf_op jit(solution)/shard_map/ppermute | solution.py:23
  71.5 26.7 %all-to-all-start.1 = ((f16[8,32,2688]{2,1,0:T(8,128)(2,1)}), f16[8,32,2688]{2,1,0:T(8,128)(2,1)}, u32[]{:S(2)}, u32[]{:S(2)}) async-start(f16[8,32,2688]{2,1,0:T(8,128)(2,1)} %convert_element_type.25), calls=%async_computation.1 | async-start | bytes 2752512 | tf_op jit(solution)/shard_map/all_to_all | solution.py:203
  101.7 22.7 %all-to-all-start.2 = ((f16[8,32,2048]{2,1,0:T(8,128)(2,1)}), f16[8,32,2048]{2,1,0:T(8,128)(2,1)S(1)}, u32[]{:S(2)}, u32[]{:S(2)}) async-start(f16[8,32,2048]{2,1,0:T(8,128)(2,1)} %convert_element_type.27), calls=%async_computation.2 | async-start | bytes 2097152 | tf_op jit(solution)/shard_map/all_to_all | solution.py:203
  105.2 21.6 %collective-permute-start.10 = (f32[32,1024]{1,0:T(8,128)S(1)}, f32[32,1024]{1,0:T(8,128)S(1)}, u32[]{:S(2)}, u32[]{:S(2)}) collective-permute-start(f32[32,1024]{1,0:T(8,128)S(1)} %get-tuple-element.18), channel_id=1, source_target_pairs={{0,232},{8,224},{16,248},{24,240},{32,8},{40,0},{48,24},{56,16},{6... | collective-permute-start | bytes 393224 | tf_op jit(solution)/shard_map/ppermute | solution.py:23
  106.5 21.4 %collective-permute-start.11 = (f32[32,1024]{1,0:T(8,128)S(1)}, f32[32,1024]{1,0:T(8,128)S(1)}, u32[]{:S(2)}, u32[]{:S(2)}) collective-permute-start(f32[32,1024]{1,0:T(8,128)S(1)} %get-tuple-element.19), channel_id=1, source_target_pairs={{0,48},{8,56},{16,32},{24,40},{32,80},{40,88},{48,64},{56,72},{64,... | collective-permute-start | bytes 393224 | tf_op jit(solution)/shard_map/ppermute | solution.py:23
  107.9 23.4 %collective-permute-start.12 = (f32[32,1024]{1,0:T(8,128)S(1)}, f32[32,1024]{1,0:T(8,128)S(1)}, u32[]{:S(2)}, u32[]{:S(2)}) collective-permute-start(f32[32,1024]{1,0:T(8,128)S(1)} %get-tuple-element.20), channel_id=1, source_target_pairs={{0,56},{8,48},{16,40},{24,32},{32,88},{40,80},{48,72},{56,64},{64,... | collective-permute-start | bytes 393224 | tf_op jit(solution)/shard_map/ppermute | solution.py:23
  110.9 21.2 %collective-permute-start.9 = (f32[32,1024]{1,0:T(8,128)S(1)}, f32[32,1024]{1,0:T(8,128)S(1)}, u32[]{:S(2)}, u32[]{:S(2)}) collective-permute-start(f32[32,1024]{1,0:T(8,128)S(1)} %get-tuple-element.17), channel_id=1, source_target_pairs={{0,224},{8,232},{16,240},{24,248},{32,0},{40,8},{48,16},{56,24},{6... | collective-permute-start | bytes 393224 | tf_op jit(solution)/shard_map/ppermute | solution.py:23
  124.5 13.5 %copy-start.10 = (s32[32]{0:T(128)S(1)}, s32[32]{0:T(128)}, u32[]{:S(2)}) copy-start(s32[32]{0:T(128)} %constant.54.clone) | copy-start | bytes 388
  125.0 13.0 %collective-permute-start.13 = (f32[32,512]{1,0:T(8,128)S(1)}, f32[32,512]{1,0:T(8,128)S(1)}, u32[]{:S(2)}, u32[]{:S(2)}) collective-permute-start(f32[32,512]{1,0:T(8,128)S(1)} %get-tuple-element.23), channel_id=1, source_target_pairs={{0,32},{8,40},{16,48},{24,56},{32,64},{40,72},{48,80},{56,88},{64,... | collective-permute-start | bytes 196616 | tf_op jit(solution)/shard_map/ppermute | solution.py:23
  126.8 11.2 %collective-permute-start.14 = (f32[32,512]{1,0:T(8,128)S(1)}, f32[32,512]{1,0:T(8,128)S(1)}, u32[]{:S(2)}, u32[]{:S(2)}) collective-permute-start(f32[32,512]{1,0:T(8,128)S(1)} %get-tuple-element.24), channel_id=1, source_target_pairs={{0,224},{8,232},{16,240},{24,248},{32,0},{40,8},{48,16},{56,24},{6... | collective-permute-start | bytes 196616 | tf_op jit(solution)/shard_map/ppermute | solution.py:23
  127.9 10.1 %collective-permute-start.15 = (f32[32,512]{1,0:T(8,128)S(1)}, f32[32,512]{1,0:T(8,128)S(1)}, u32[]{:S(2)}, u32[]{:S(2)}) collective-permute-start(f32[32,512]{1,0:T(8,128)S(1)} %get-tuple-element.25), channel_id=1, source_target_pairs={{0,64},{8,72},{16,80},{24,88},{32,96},{40,104},{48,112},{56,120},{... | collective-permute-start | bytes 196616 | tf_op jit(solution)/shard_map/ppermute | solution.py:23
  131.3 6.8 %collective-permute-start.16 = (f32[32,512]{1,0:T(8,128)S(1)}, f32[32,512]{1,0:T(8,128)S(1)}, u32[]{:S(2)}, u32[]{:S(2)}) collective-permute-start(f32[32,512]{1,0:T(8,128)S(1)} %get-tuple-element.26), channel_id=1, source_target_pairs={{0,192},{8,200},{16,208},{24,216},{32,224},{40,232},{48,240},{56,2... | collective-permute-start | bytes 196616 | tf_op jit(solution)/shard_map/ppermute | solution.py:23
  132.1 7.9 %collective-permute-start.17 = (f32[32,512]{1,0:T(8,128)S(1)}, f32[32,512]{1,0:T(8,128)S(1)}, u32[]{:S(2)}, u32[]{:S(2)}) collective-permute-start(f32[32,512]{1,0:T(8,128)S(1)} %get-tuple-element.27), channel_id=1, source_target_pairs={{0,96},{8,104},{16,112},{24,120},{32,128},{40,136},{48,144},{56,15... | collective-permute-start | bytes 196616 | tf_op jit(solution)/shard_map/ppermute | solution.py:23
  138.0 7.7 %collective-permute-start.18 = (f32[32,512]{1,0:T(8,128)S(1)}, f32[32,512]{1,0:T(8,128)S(1)}, u32[]{:S(2)}, u32[]{:S(2)}) collective-permute-start(f32[32,512]{1,0:T(8,128)S(1)} %get-tuple-element.28), channel_id=1, source_target_pairs={{0,160},{8,168},{16,176},{24,184},{32,192},{40,200},{48,208},{56,2... | collective-permute-start | bytes 196616 | tf_op jit(solution)/shard_map/ppermute | solution.py:23
  (10 other events, 41.9 us)

commit v5 on v4

--- a/solution.py
+++ b/solution.py
@@ -88,23 +88,26 @@
     return sums
 
 
-def turn_kernel(first_ref, second_ref, last_ref, own_ref, core_ref, half_ref, cross_ref, out_ref):
+def turn_kernel(zero_ref, first_ref, second_ref, last_ref, own_ref, core_ref, half_ref, cross_ref, diagonal_ref, side_ref, out_ref):
     ndest, part, ahead = last_ref.shape
     width = ndest * part
-    first = summed(first_ref, 0, 6, 6 * width)
+    zero = summed(zero_ref, 0, 2, 2 * width)
+    first = summed(first_ref, 0, 4, 4 * width)
     second = summed(second_ref, 0, 10, 10 * width)
     for ref, blocks in (
-        (own_ref, first[:3] + second[:1]),
-        (core_ref, first[3:] + second[1:2]),
+        (own_ref, first[:2] + second[:1]),
+        (core_ref, first[2:] + second[1:2]),
         (half_ref, second[2:6]),
         (cross_ref, second[6:]),
+        (diagonal_ref, zero[:1]),
+        (side_ref, zero[1:]),
     ):
         for at, block in enumerate(blocks):
             ref[:, at * width : (at + 1) * width] = block
     out_ref[:, :, :ahead] = last_ref[...]
     groups = (
-        (first[1], first[4], second[3], second[7]),
-        (first[2], first[5], second[4], second[8]),
+        (first[0], first[2], second[3], second[7]),
+        (first[1], first[3], second[4], second[8]),
         (second[0], second[1], second[5], second[9]),
     )
     groups = [jnp.concatenate(group, axis=0) for group in groups]
@@ -120,17 +123,17 @@
     out_ref[:, :, ahead + 6 * step :] = jnp.broadcast_to(power.reshape(1, 1, 1), (ndest, part, LANES))
 
 
-def turn(first, second, last):
+def turn(zero, first, second, last):
     ndest, part, ahead = last.shape
     width = ndest * part
-    bundle = jax.ShapeDtypeStruct((part, 4 * width), jnp.float32)
+    bundles = [jax.ShapeDtypeStruct((part, count * width), jnp.float32) for count in (3, 3, 4, 4, 1, 1)]
     return pl.pallas_call(
         turn_kernel,
-        in_specs=[VMEM] * 3,
-        out_specs=[VMEM] * 5,
-        out_shape=[bundle] * 4 + [jax.ShapeDtypeStruct((ndest, part, ahead + 24 * part + LANES), jnp.float32)],
-        compiler_params=ROOM,
-    )(first, second, last)
+        in_specs=[VMEM] * 4,
+        out_specs=[VMEM] * 7,
+        out_shape=bundles + [jax.ShapeDtypeStruct((ndest, part, ahead + 24 * part + LANES), jnp.float32)],
+        compiler_params=ROOM,
+    )(zero, first, second, last)
 
 
 def settle_kernel(in_ref, *outs):
@@ -203,12 +206,15 @@
         return lax.all_to_all(parts, "col", 0, 0, tiled=True)
 
     up1, down1 = shift(gradient, dz=-1), shift(gradient, dz=1)
+    core0 = shift(gradient, dc=1)
+    zero = tiles([gradient, core0], [gradient], [(0, 0), (1, 0)], ncol, scaled=True)
+    zero = exchange(zero.astype(jnp.float16))
     half1 = shift(up1, dy=1)
-    core1 = shift(down1, dc=1)
+    core1 = shift(hold(down1, zero, up1), dc=1)
     up2, down2 = shift(up1, dz=-1), shift(down1, dz=1)
 
-    near = [(row, column) for row in range(2) for column in range(3)]
-    first = tiles([down1, core1], [down1, gradient, up1], near, ncol, scaled=True)
+    near = [(row, column) for row in range(2) for column in range(2)]
+    first = tiles([down1, core1], [gradient, up1], near, ncol, scaled=True)
     first = exchange(first.astype(jnp.float16))
     half1 = hold(half1, first)
     cross1 = shift(half1, dc=1)
@@ -217,7 +223,9 @@
     second = tiles([down1, core1, half1, cross1], [up2, up1, gradient, down1, down2], middle, ncol, scaled=True)
     second = exchange(second.astype(jnp.float16))
     last = tiles([up3, down3], [down1, core1, half1, cross1], [(0, 0), (0, 1), (1, 2), (1, 3)], ncol, scaled=True, weigh=40)
-    own, core, half, cross, last = turn(first.astype(jnp.float32), second.astype(jnp.float32), last)
+    own, core, half, cross, diagonal, side, last = turn(
+        zero.astype(jnp.float32), first.astype(jnp.float32), second.astype(jnp.float32), last
+    )
     last = exchange(last.astype(jnp.float16))
 
     home = [
@@ -225,8 +233,11 @@
         shift(core, dz=-1, dc=1),
         shift(half, dz=1, dy=1),
         shift(cross, dz=1, dy=1, dc=1),
+        diagonal,
+        shift(side, dc=1),
     ]
-    home_labels = [(k, d if k < 2 else -d) for k in range(4) for d in range(4)]
+    home_labels = [(k, d) for k in range(2) for d in range(1, 4)] + [(k, -d) for k in (2, 3) for d in range(4)]
+    home_labels += [(0, 0), (1, 0)]
     still, above1, below1, above2, below2, above3, below3 = settle(last.astype(jnp.float32))
     away = [
         still,

time: 148 us -> 147 us (level)
  waiting for transfers between devices: 75.8 us -> 65.8 us
  starting transfers between devices: 44.6 us -> 49.2 us
  other arithmetic: 7.64 us -> 9.17 us
    ppermute x19 -> x21, waiting for transfers between devices: 39.6 us -> 30.6 us  [shift(): return lax.ppermute(value, 'row', pairs)]
    all_to_all x3 -> x4, starting transfers between devices: 13.1 us -> 18.7 us  [exchange(): return lax.all_to_all(parts, 'col', 0, 0, tiled=True)]
    convert_element_type x0 -> x2, other arithmetic: none -> 1.68 us  [the longest x1 0.92 us: per_device(): zero.astype(jnp.float32)]
    ppermute x19 -> x21, starting transfers between devices: 31.6 us -> 30.5 us  [shift(): return lax.ppermute(value, 'row', pairs)]
    all_to_all x3 -> x4, waiting for transfers between devices: 36.2 us -> 35.1 us  [exchange(): return lax.all_to_all(parts, 'col', 0, 0, tiled=True)]
    pallas_call x3 -> x4, Pallas kernels: 8.9 us -> 9.21 us  [tiles(): pl.pallas_call(lambda *refs: tiles_kernel(len(lefts), len(rights), pairs,...]
    unnamed x24 -> x38, local copies, waits for them, and re-layouts: 5.56 us -> 5.65 us
  transfers between devices with their start and end apart: 22 -> 25, of which waited for: 9 -> 10; matrix products, arithmetic and copies ran while one was open for 4% -> 6% of each run, Pallas kernels for 6% -> 7%
where the time goes in v5:
time: 147 us; the launch traced here: 146 us
  waiting for transfers between devices  65.8 us (45%)
  starting transfers between devices  49.2 us (33%)
  Pallas kernels  12 us (8%)
  other arithmetic  9.17 us (6%)
  local copies, waits for them, and re-layouts  7.32 us (5%)
  between operations  2.28 us (2%)
    all_to_all x4, waiting for transfers between devices, exchange(): return lax.all_to_all(parts, 'col', 0, 0, tiled=True)  35.1 us
    ppermute x21, waiting for transfers between devices, shift(): return lax.ppermute(value, 'row', pairs)  30.6 us
    ppermute x21, starting transfers between devices, shift(): return lax.ppermute(value, 'row', pairs)  30.5 us
    all_to_all x4, starting transfers between devices, exchange(): return lax.all_to_all(parts, 'col', 0, 0, tiled=True)  18.7 us
    pallas_call x4, Pallas kernels, tiles(): pl.pallas_call(lambda *refs: tiles_kernel(len(lefts), len(rights), pairs,...  9.21 us
    unnamed x38, local copies, waits for them, and re-layouts  5.65 us
  transfers between devices with their start and end apart: 25, of which 10 were waited for; matrix products, arithmetic and copies ran while one was open for 6% of the time, Pallas kernels for 7%

profile of v5, /device:TPU:32, one launch (start us, length us, event | category | flops | bytes accessed | tf_op | source)
XLA Modules:
  0.0 145.8 jit_solution(8763527949958582122)
XLA Ops:
  0.0 1.8 %collective-permute-start.2 = (bf16[256,1792]{1,0:T(8,128)(2,1)}, bf16[256,1792]{1,0:T(8,128)(2,1)S(1)}, u32[]{:S(2)}, u32[]{:S(2)}) collective-permute-start(bf16[256,1792]{1,0:T(8,128)(2,1)} %refs_6_.1), channel_id=1, source_target_pairs={{0,224},{8,232},{16,240},{24,248},{32,0},{40,8},{48,16},{56,24},{6... | collective-permute-start | bytes 2752520 | tf_op jit(solution)/shard_map/ppermute | solution.py:23
  5.4 5.4 %all-to-all-start = ((f16[8,32,640]{2,1,0:T(8,128)(2,1)}), f16[8,32,640]{2,1,0:T(8,128)(2,1)S(1)}, u32[]{:S(2)}, u32[]{:S(2)}) async-start(f16[8,32,640]{2,1,0:T(8,128)(2,1)} %convert_element_type.32), calls=%async_computation | async-start | bytes 655360 | tf_op jit(solution)/shard_map/all_to_all | solution.py:206
  10.9 12.3 %collective-permute-done.2.refs_3_.refs_5_ = bf16[256,1792]{1,0:T(8,128)(2,1)S(1)} collective-permute-done((bf16[256,1792]{1,0:T(8,128)(2,1)}, bf16[256,1792]{1,0:T(8,128)(2,1)S(1)}, u32[]{:S(2)}, u32[]{:S(2)}) %collective-permute-start.2) | collective-permute-done | bytes 917536 | tf_op jit(solution)/shard_map/ppermute | solution.py:23
  27.1 3.3 %collective-permute-start.4 = (bf16[256,1792]{1,0:T(8,128)(2,1)S(1)}, bf16[256,1792]{1,0:T(8,128)(2,1)}, u32[]{:S(2)}, u32[]{:S(2)}) collective-permute-start(bf16[256,1792]{1,0:T(8,128)(2,1)S(1)} %collective-permute-done.2.refs_3_.refs_5_), channel_id=1, source_target_pairs={{0,16},{8,24},{16,0},{24,8},{32,48},{40,56},{48,32},{56,40},{64,80... | collective-permute-start | bytes 2752520 | tf_op jit(solution)/shard_map/ppermute | solution.py:23
  32.7 4.5 %all-to-all-start.1 = ((f16[8,32,1152]{2,1,0:T(8,128)(2,1)}), f16[8,32,1152]{2,1,0:T(8,128)(2,1)S(1)}, u32[]{:S(2)}, u32[]{:S(2)}) async-start(f16[8,32,1152]{2,1,0:T(8,128)(2,1)} %convert_element_type.35), calls=%async_computation.1 | async-start | bytes 1179648 | tf_op jit(solution)/shard_map/all_to_all | solution.py:206
  37.2 3.0 %collective-permute-start.6 = (bf16[256,1792]{1,0:T(8,128)(2,1)S(1)}, bf16[256,1792]{1,0:T(8,128)(2,1)}, u32[]{:S(2)}, u32[]{:S(2)}) collective-permute-start(bf16[256,1792]{1,0:T(8,128)(2,1)S(1)} %collective-permute-done.2.refs_3_.refs_5_), channel_id=1, source_target_pairs={{0,224},{8,232},{16,240},{24,248},{32,0},{40,8},{48,16},{56,24},{6... | collective-permute-start | bytes 2752520 | tf_op jit(solution)/shard_map/ppermute | solution.py:23
  40.2 17.9 %all-to-all-done.1 = f16[8,32,1152]{2,1,0:T(8,128)(2,1)S(1)} async-done(((f16[8,32,1152]{2,1,0:T(8,128)(2,1)}), f16[8,32,1152]{2,1,0:T(8,128)(2,1)S(1)}, u32[]{:S(2)}, u32[]{:S(2)}) %all-to-all-start.1) | async-done | bytes 589856 | tf_op jit(solution)/shard_map/all_to_all | solution.py:206
  60.6 3.0 %collective-permute-start.8 = (bf16[256,1792]{1,0:T(8,128)(2,1)}, bf16[256,1792]{1,0:T(8,128)(2,1)}, u32[]{:S(2)}, u32[]{:S(2)}) collective-permute-start(bf16[256,1792]{1,0:T(8,128)(2,1)} %collective-permute-done.6.refs_4_), channel_id=1, source_target_pairs={{0,224},{8,232},{16,240},{24,248},{32,0},{40,8},{48,16},{56,24},{6... | collective-permute-start | bytes 2752520 | tf_op jit(solution)/shard_map/ppermute | solution.py:23
  65.7 4.3 %shard_map.39 = f32[8,32,2688]{2,1,0:T(8,128)S(1)} custom-call(bf16[256,1792]{1,0:T(8,128)(2,1)S(1)} %collective-permute-done.1.refs_0_.refs_7_.refs_2_, bf16[256,1792]{1,0:T(8,128)(2,1)S(1)} %copy-done.5, bf16[256,1792]{1,0:T(8,128)(2,1)S(1)} %broadcast_add_fusion.refs_2_.refs_4_, bf16[256,1792]{1,0:T(8,128)(2,1)S(1)} %collective-permute-done.5.refs_3_.refs_5_, ...), custom_call_target="tpu_custom_call" | custom-call | flops 2348810240 | bytes 10878976 | tf_op jit(solution)/shard_map/pallas_call | solution.py:57
  72.3 5.2 %all-to-all-start.2 = ((f16[8,32,2688]{2,1,0:T(8,128)(2,1)}), f16[8,32,2688]{2,1,0:T(8,128)(2,1)}, u32[]{:S(2)}, u32[]{:S(2)}) async-start(f16[8,32,2688]{2,1,0:T(8,128)(2,1)} %convert_element_type.38), calls=%async_computation.2 | async-start | bytes 2752512 | tf_op jit(solution)/shard_map/all_to_all | solution.py:206
  77.5 6.6 %collective-permute-done.8.refs_0_ = bf16[256,1792]{1,0:T(8,128)(2,1)} collective-permute-done((bf16[256,1792]{1,0:T(8,128)(2,1)}, bf16[256,1792]{1,0:T(8,128)(2,1)}, u32[]{:S(2)}, u32[]{:S(2)}) %collective-permute-start.8) | collective-permute-done | bytes 917536 | tf_op jit(solution)/shard_map/ppermute | solution.py:23
  84.1 3.3 %collective-permute-done.9.refs_1_ = bf16[256,1792]{1,0:T(8,128)(2,1)} collective-permute-done((bf16[256,1792]{1,0:T(8,128)(2,1)}, bf16[256,1792]{1,0:T(8,128)(2,1)}, u32[]{:S(2)}, u32[]{:S(2)}) %collective-permute-start.9) | collective-permute-done | bytes 917536 | tf_op jit(solution)/shard_map/ppermute | solution.py:23
  89.8 2.8 %shard_map.40.last_ref = f32[8,32,1152]{2,1,0:T(8,128)S(1)} custom-call(bf16[256,1792]{1,0:T(8,128)(2,1)} %collective-permute-done.8.refs_0_, bf16[256,1792]{1,0:T(8,128)(2,1)} %collective-permute-done.9.refs_1_, bf16[256,1792]{1,0:T(8,128)(2,1)S(1)} %collective-permute-done.1.refs_0_.refs_7_.refs_2_, bf16[256,1792]{1,0:T(8,128)(2,1)S(1)} %copy-done.6, ...), custom_call_target="tpu_custom_call" | custom-call | flops 37580963840 | bytes 6553600 | tf_op jit(solution)/shard_map/pallas_call | solution.py:57
  93.6 5.5 %all-to-all-done.2 = f16[8,32,2688]{2,1,0:T(8,128)(2,1)} async-done(((f16[8,32,2688]{2,1,0:T(8,128)(2,1)}), f16[8,32,2688]{2,1,0:T(8,128)(2,1)}, u32[]{:S(2)}, u32[]{:S(2)}) %all-to-all-start.2) | async-done | bytes 1376288 | tf_op jit(solution)/shard_map/all_to_all | solution.py:206
  102.5 3.6 %all-to-all-start.3 = ((f16[8,32,2048]{2,1,0:T(8,128)(2,1)}), f16[8,32,2048]{2,1,0:T(8,128)(2,1)S(1)}, u32[]{:S(2)}, u32[]{:S(2)}) async-start(f16[8,32,2048]{2,1,0:T(8,128)(2,1)} %convert_element_type.40), calls=%async_computation.3 | async-start | bytes 2097152 | tf_op jit(solution)/shard_map/all_to_all | solution.py:206
  106.3 3.6 %collective-permute-start.13 = (f32[32,1024]{1,0:T(8,128)S(1)}, f32[32,1024]{1,0:T(8,128)S(1)}, u32[]{:S(2)}, u32[]{:S(2)}) collective-permute-start(f32[32,1024]{1,0:T(8,128)S(1)} %get-tuple-element.22), channel_id=1, source_target_pairs={{0,56},{8,48},{16,40},{24,32},{32,88},{40,80},{48,72},{56,64},{64,... | collective-permute-start | bytes 393224 | tf_op jit(solution)/shard_map/ppermute | solution.py:23
  109.9 3.3 %collective-permute-start.11 = (f32[32,768]{1,0:T(8,128)S(1)}, f32[32,768]{1,0:T(8,128)S(1)}, u32[]{:S(2)}, u32[]{:S(2)}) collective-permute-start(f32[32,768]{1,0:T(8,128)S(1)} %get-tuple-element.20), channel_id=1, source_target_pairs={{0,232},{8,224},{16,248},{24,240},{32,8},{40,0},{48,24},{56,16},{6... | collective-permute-start | bytes 294920 | tf_op jit(solution)/shard_map/ppermute | solution.py:23
  113.3 11.7 %all-to-all-done.3 = f16[8,32,2048]{2,1,0:T(8,128)(2,1)S(1)} async-done(((f16[8,32,2048]{2,1,0:T(8,128)(2,1)}), f16[8,32,2048]{2,1,0:T(8,128)(2,1)S(1)}, u32[]{:S(2)}, u32[]{:S(2)}) %all-to-all-start.3) | async-done | bytes 1048608 | tf_op jit(solution)/shard_map/all_to_all | solution.py:206
  126.2 2.2 %collective-permute-start.16 = (f32[32,512]{1,0:T(8,128)S(1)}, f32[32,512]{1,0:T(8,128)S(1)}, u32[]{:S(2)}, u32[]{:S(2)}) collective-permute-start(f32[32,512]{1,0:T(8,128)S(1)} %get-tuple-element.28), channel_id=1, source_target_pairs={{0,224},{8,232},{16,240},{24,248},{32,0},{40,8},{48,16},{56,24},{6... | collective-permute-start | bytes 196616 | tf_op jit(solution)/shard_map/ppermute | solution.py:23
  129.4 3.2 %collective-permute-start.18 = (f32[32,512]{1,0:T(8,128)S(1)}, f32[32,512]{1,0:T(8,128)S(1)}, u32[]{:S(2)}, u32[]{:S(2)}) collective-permute-start(f32[32,512]{1,0:T(8,128)S(1)} %get-tuple-element.30), channel_id=1, source_target_pairs={{0,192},{8,200},{16,208},{24,216},{32,224},{40,232},{48,240},{56,2... | collective-permute-start | bytes 196616 | tf_op jit(solution)/shard_map/ppermute | solution.py:23
  132.6 3.3 %collective-permute-start.19 = (f32[32,512]{1,0:T(8,128)S(1)}, f32[32,512]{1,0:T(8,128)S(1)}, u32[]{:S(2)}, u32[]{:S(2)}) collective-permute-start(f32[32,512]{1,0:T(8,128)S(1)} %get-tuple-element.31), channel_id=1, source_target_pairs={{0,96},{8,104},{16,112},{24,120},{32,128},{40,136},{48,144},{56,15... | collective-permute-start | bytes 196616 | tf_op jit(solution)/shard_map/ppermute | solution.py:23
  135.8 1.8 %collective-permute-start.20 = (f32[32,512]{1,0:T(8,128)S(1)}, f32[32,512]{1,0:T(8,128)S(1)}, u32[]{:S(2)}, u32[]{:S(2)}) collective-permute-start(f32[32,512]{1,0:T(8,128)S(1)} %get-tuple-element.32), channel_id=1, source_target_pairs={{0,160},{8,168},{16,176},{24,184},{32,192},{40,200},{48,208},{56,2... | collective-permute-start | bytes 196616 | tf_op jit(solution)/shard_map/ppermute | solution.py:23
  137.6 2.9 %collective-permute-done.19.refs_11_ = f32[32,512]{1,0:T(8,128)S(1)} collective-permute-done((f32[32,512]{1,0:T(8,128)S(1)}, f32[32,512]{1,0:T(8,128)S(1)}, u32[]{:S(2)}, u32[]{:S(2)}) %collective-permute-start.19) | collective-permute-done | bytes 65568 | tf_op jit(solution)/shard_map/ppermute | solution.py:23
  140.5 3.6 %collective-permute-done.20.refs_12_ = f32[32,512]{1,0:T(8,128)S(1)} collective-permute-done((f32[32,512]{1,0:T(8,128)S(1)}, f32[32,512]{1,0:T(8,128)S(1)}, u32[]{:S(2)}, u32[]{:S(2)}) %collective-permute-start.20) | collective-permute-done | bytes 65568 | tf_op jit(solution)/shard_map/ppermute | solution.py:23
  (85 shorter events, 25.4 us)
Async XLA Ops:
  0.0 23.1 %collective-permute-start.2 = (bf16[256,1792]{1,0:T(8,128)(2,1)}, bf16[256,1792]{1,0:T(8,128)(2,1)S(1)}, u32[]{:S(2)}, u32[]{:S(2)}) collective-permute-start(bf16[256,1792]{1,0:T(8,128)(2,1)} %refs_6_.1), channel_id=1, source_target_pairs={{0,224},{8,232},{16,240},{24,248},{32,0},{40,8},{48,16},{56,24},{6... | collective-permute-start | bytes 2752520 | tf_op jit(solution)/shard_map/ppermute | solution.py:23
  1.8 25.1 %collective-permute-start.1 = (bf16[256,1792]{1,0:T(8,128)(2,1)}, bf16[256,1792]{1,0:T(8,128)(2,1)S(1)}, u32[]{:S(2)}, u32[]{:S(2)}) collective-permute-start(bf16[256,1792]{1,0:T(8,128)(2,1)} %refs_6_.1), channel_id=1, source_target_pairs={{0,32},{8,40},{16,48},{24,56},{32,64},{40,72},{48,80},{56,88},{64,... | collective-permute-start | bytes 2752520 | tf_op jit(solution)/shard_map/ppermute | solution.py:23
  5.4 19.0 %all-to-all-start = ((f16[8,32,640]{2,1,0:T(8,128)(2,1)}), f16[8,32,640]{2,1,0:T(8,128)(2,1)S(1)}, u32[]{:S(2)}, u32[]{:S(2)}) async-start(f16[8,32,640]{2,1,0:T(8,128)(2,1)} %convert_element_type.32), calls=%async_computation | async-start | bytes 655360 | tf_op jit(solution)/shard_map/all_to_all | solution.py:206
  27.0 3.4 %collective-permute-start.3 = (bf16[256,1792]{1,0:T(8,128)(2,1)S(1)}, bf16[256,1792]{1,0:T(8,128)(2,1)S(1)}, u32[]{:S(2)}, u32[]{:S(2)}) collective-permute-start(bf16[256,1792]{1,0:T(8,128)(2,1)S(1)} %add_add_fusion), channel_id=1, source_target_pairs={{0,8},{8,0},{16,24},{24,16},{32,40},{40,32},{48,56},{56,48},{64,72... | collective-permute-start | bytes 2752520 | tf_op jit(solution)/shard_map/ppermute | solution.py:23
  27.1 32.1 %collective-permute-start.4 = (bf16[256,1792]{1,0:T(8,128)(2,1)S(1)}, bf16[256,1792]{1,0:T(8,128)(2,1)}, u32[]{:S(2)}, u32[]{:S(2)}) collective-permute-start(bf16[256,1792]{1,0:T(8,128)(2,1)S(1)} %collective-permute-done.2.refs_3_.refs_5_), channel_id=1, source_target_pairs={{0,16},{8,24},{16,0},{24,8},{32,48},{40,56},{48,32},{56,40},{64,80... | collective-permute-start | bytes 2752520 | tf_op jit(solution)/shard_map/ppermute | solution.py:23
  32.7 25.4 %all-to-all-start.1 = ((f16[8,32,1152]{2,1,0:T(8,128)(2,1)}), f16[8,32,1152]{2,1,0:T(8,128)(2,1)S(1)}, u32[]{:S(2)}, u32[]{:S(2)}) async-start(f16[8,32,1152]{2,1,0:T(8,128)(2,1)} %convert_element_type.35), calls=%async_computation.1 | async-start | bytes 1179648 | tf_op jit(solution)/shard_map/all_to_all | solution.py:206
  37.2 23.4 %collective-permute-start.6 = (bf16[256,1792]{1,0:T(8,128)(2,1)S(1)}, bf16[256,1792]{1,0:T(8,128)(2,1)}, u32[]{:S(2)}, u32[]{:S(2)}) collective-permute-start(bf16[256,1792]{1,0:T(8,128)(2,1)S(1)} %collective-permute-done.2.refs_3_.refs_5_), channel_id=1, source_target_pairs={{0,224},{8,232},{16,240},{24,248},{32,0},{40,8},{48,16},{56,24},{6... | collective-permute-start | bytes 2752520 | tf_op jit(solution)/shard_map/ppermute | solution.py:23
  40.2 23.4 %collective-permute-start.7 = (bf16[256,1792]{1,0:T(8,128)(2,1)S(1)}, bf16[256,1792]{1,0:T(8,128)(2,1)}, u32[]{:S(2)}, u32[]{:S(2)}) collective-permute-start(bf16[256,1792]{1,0:T(8,128)(2,1)S(1)} %collective-permute-done.1.refs_0_.refs_7_.refs_2_), channel_id=1, source_target_pairs={{0,32},{8,40},{16,48},{24,56},{32,64},{40,72},{48,80},{56,88},{64,... | collective-permute-start | bytes 2752520 | tf_op jit(solution)/shard_map/ppermute | solution.py:23
  60.5 5.2 %collective-permute-start.5 = (bf16[256,1792]{1,0:T(8,128)(2,1)S(1)}, bf16[256,1792]{1,0:T(8,128)(2,1)S(1)}, u32[]{:S(2)}, u32[]{:S(2)}) collective-permute-start(bf16[256,1792]{1,0:T(8,128)(2,1)S(1)} %broadcast_add_fusion.refs_2_.refs_4_), channel_id=1, source_target_pairs={{0,8},{8,0},{16,24},{24,16},{32,40},{40,32},{48,56},{56,48},{64,72... | collective-permute-start | bytes 2752520 | tf_op jit(solution)/shard_map/ppermute | solution.py:23
  60.6 23.5 %collective-permute-start.8 = (bf16[256,1792]{1,0:T(8,128)(2,1)}, bf16[256,1792]{1,0:T(8,128)(2,1)}, u32[]{:S(2)}, u32[]{:S(2)}) collective-permute-start(bf16[256,1792]{1,0:T(8,128)(2,1)} %collective-permute-done.6.refs_4_), channel_id=1, source_target_pairs={{0,224},{8,232},{16,240},{24,248},{32,0},{40,8},{48,16},{56,24},{6... | collective-permute-start | bytes 2752520 | tf_op jit(solution)/shard_map/ppermute | solution.py:23
  63.6 23.8 %collective-permute-start.9 = (bf16[256,1792]{1,0:T(8,128)(2,1)}, bf16[256,1792]{1,0:T(8,128)(2,1)}, u32[]{:S(2)}, u32[]{:S(2)}) collective-permute-start(bf16[256,1792]{1,0:T(8,128)(2,1)} %collective-permute-done.7.refs_8_), channel_id=1, source_target_pairs={{0,32},{8,40},{16,48},{24,56},{32,64},{40,72},{48,80},{56,88},{64,... | collective-permute-start | bytes 2752520 | tf_op jit(solution)/shard_map/ppermute | solution.py:23
  72.3 26.8 %all-to-all-start.2 = ((f16[8,32,2688]{2,1,0:T(8,128)(2,1)}), f16[8,32,2688]{2,1,0:T(8,128)(2,1)}, u32[]{:S(2)}, u32[]{:S(2)}) async-start(f16[8,32,2688]{2,1,0:T(8,128)(2,1)} %convert_element_type.38), calls=%async_computation.2 | async-start | bytes 2752512 | tf_op jit(solution)/shard_map/all_to_all | solution.py:206
  102.5 22.5 %all-to-all-start.3 = ((f16[8,32,2048]{2,1,0:T(8,128)(2,1)}), f16[8,32,2048]{2,1,0:T(8,128)(2,1)S(1)}, u32[]{:S(2)}, u32[]{:S(2)}) async-start(f16[8,32,2048]{2,1,0:T(8,128)(2,1)} %convert_element_type.40), calls=%async_computation.3 | async-start | bytes 2097152 | tf_op jit(solution)/shard_map/all_to_all | solution.py:206
  106.1 23.3 %collective-permute-start.12 = (f32[32,1024]{1,0:T(8,128)S(1)}, f32[32,1024]{1,0:T(8,128)S(1)}, u32[]{:S(2)}, u32[]{:S(2)}) collective-permute-start(f32[32,1024]{1,0:T(8,128)S(1)} %get-tuple-element.21), channel_id=1, source_target_pairs={{0,48},{8,56},{16,32},{24,40},{32,80},{40,88},{48,64},{56,72},{64,... | collective-permute-start | bytes 393224 | tf_op jit(solution)/shard_map/ppermute | solution.py:23
  106.3 26.3 %collective-permute-start.13 = (f32[32,1024]{1,0:T(8,128)S(1)}, f32[32,1024]{1,0:T(8,128)S(1)}, u32[]{:S(2)}, u32[]{:S(2)}) collective-permute-start(f32[32,1024]{1,0:T(8,128)S(1)} %get-tuple-element.22), channel_id=1, source_target_pairs={{0,56},{8,48},{16,40},{24,32},{32,88},{40,80},{48,72},{56,64},{64,... | collective-permute-start | bytes 393224 | tf_op jit(solution)/shard_map/ppermute | solution.py:23
  109.9 16.3 %collective-permute-start.10 = (f32[32,768]{1,0:T(8,128)S(1)}, f32[32,768]{1,0:T(8,128)S(1)}, u32[]{:S(2)}, u32[]{:S(2)}) collective-permute-start(f32[32,768]{1,0:T(8,128)S(1)} %get-tuple-element.19), channel_id=1, source_target_pairs={{0,224},{8,232},{16,240},{24,248},{32,0},{40,8},{48,16},{56,24},{6... | collective-permute-start | bytes 294920 | tf_op jit(solution)/shard_map/ppermute | solution.py:23
  109.9 18.5 %collective-permute-start.11 = (f32[32,768]{1,0:T(8,128)S(1)}, f32[32,768]{1,0:T(8,128)S(1)}, u32[]{:S(2)}, u32[]{:S(2)}) collective-permute-start(f32[32,768]{1,0:T(8,128)S(1)} %get-tuple-element.20), channel_id=1, source_target_pairs={{0,232},{8,224},{16,248},{24,240},{32,8},{40,0},{48,24},{56,16},{6... | collective-permute-start | bytes 294920 | tf_op jit(solution)/shard_map/ppermute | solution.py:23
  113.3 12.4 %collective-permute-start.14 = (f32[32,256]{1,0:T(8,128)S(1)}, f32[32,256]{1,0:T(8,128)S(1)}, u32[]{:S(2)}, u32[]{:S(2)}) collective-permute-start(f32[32,256]{1,0:T(8,128)S(1)} %get-tuple-element.24), channel_id=1, source_target_pairs={{0,8},{8,0},{16,24},{24,16},{32,40},{40,32},{48,56},{56,48},{64,72... | collective-permute-start | bytes 98312 | tf_op jit(solution)/shard_map/ppermute | solution.py:23
  125.7 10.1 %collective-permute-start.15 = (f32[32,512]{1,0:T(8,128)S(1)}, f32[32,512]{1,0:T(8,128)S(1)}, u32[]{:S(2)}, u32[]{:S(2)}) collective-permute-start(f32[32,512]{1,0:T(8,128)S(1)} %get-tuple-element.27), channel_id=1, source_target_pairs={{0,32},{8,40},{16,48},{24,56},{32,64},{40,72},{48,80},{56,88},{64,... | collective-permute-start | bytes 196616 | tf_op jit(solution)/shard_map/ppermute | solution.py:23
  126.2 11.4 %collective-permute-start.16 = (f32[32,512]{1,0:T(8,128)S(1)}, f32[32,512]{1,0:T(8,128)S(1)}, u32[]{:S(2)}, u32[]{:S(2)}) collective-permute-start(f32[32,512]{1,0:T(8,128)S(1)} %get-tuple-element.28), channel_id=1, source_target_pairs={{0,224},{8,232},{16,240},{24,248},{32,0},{40,8},{48,16},{56,24},{6... | collective-permute-start | bytes 196616 | tf_op jit(solution)/shard_map/ppermute | solution.py:23
  128.4 9.2 %collective-permute-start.17 = (f32[32,512]{1,0:T(8,128)S(1)}, f32[32,512]{1,0:T(8,128)S(1)}, u32[]{:S(2)}, u32[]{:S(2)}) collective-permute-start(f32[32,512]{1,0:T(8,128)S(1)} %get-tuple-element.29), channel_id=1, source_target_pairs={{0,64},{8,72},{16,80},{24,88},{32,96},{40,104},{48,112},{56,120},{... | collective-permute-start | bytes 196616 | tf_op jit(solution)/shard_map/ppermute | solution.py:23
  129.4 8.3 %collective-permute-start.18 = (f32[32,512]{1,0:T(8,128)S(1)}, f32[32,512]{1,0:T(8,128)S(1)}, u32[]{:S(2)}, u32[]{:S(2)}) collective-permute-start(f32[32,512]{1,0:T(8,128)S(1)} %get-tuple-element.30), channel_id=1, source_target_pairs={{0,192},{8,200},{16,208},{24,216},{32,224},{40,232},{48,240},{56,2... | collective-permute-start | bytes 196616 | tf_op jit(solution)/shard_map/ppermute | solution.py:23
  132.6 8.0 %collective-permute-start.19 = (f32[32,512]{1,0:T(8,128)S(1)}, f32[32,512]{1,0:T(8,128)S(1)}, u32[]{:S(2)}, u32[]{:S(2)}) collective-permute-start(f32[32,512]{1,0:T(8,128)S(1)} %get-tuple-element.31), channel_id=1, source_target_pairs={{0,96},{8,104},{16,112},{24,120},{32,128},{40,136},{48,144},{56,15... | collective-permute-start | bytes 196616 | tf_op jit(solution)/shard_map/ppermute | solution.py:23
  135.8 8.3 %collective-permute-start.20 = (f32[32,512]{1,0:T(8,128)S(1)}, f32[32,512]{1,0:T(8,128)S(1)}, u32[]{:S(2)}, u32[]{:S(2)}) collective-permute-start(f32[32,512]{1,0:T(8,128)S(1)} %get-tuple-element.32), channel_id=1, source_target_pairs={{0,160},{8,168},{16,176},{24,184},{32,192},{40,200},{48,208},{56,2... | collective-permute-start | bytes 196616 | tf_op jit(solution)/shard_map/ppermute | solution.py:23
  (20 other events, 131.4 us)
